TPU v7x, 512 devices: a whole 4x8x8 slice. The times are simulated.
512 devices in a mesh: px: 32 (over x, z), py: 16 (over y, core).
Axes of the slice: x: 4, y: 8, z: 8, core: 2. Of those that a mesh axis runs over, the one named last changes fastest.
Arguments:
- field: bfloat16 [32, 256, 256, 128], P(None, 'px', 'py'), may hold values from -6 to 6
- spec_weight: bfloat16 [1, 2, 32, 32, 32, 32, 32], P(None, None, None, None, None, 'px', 'py'), may hold values from -0.5 to 0.5
- w_in: bfloat16 [1, 32, 128], replicated, may hold values from -1 to 1
- b_in: float32 [1, 128], replicated, may hold values from -4 to 4
- w_out: bfloat16 [1, 128, 32], replicated, may hold values from -0.5 to 0.5
Outputs:
- result: bfloat16 [32, 256, 256, 128], P(None, 'px', 'py')
All inputs are finite; a program needn't handle non-finite values.
Results may differ from a plain program's by a relative error of at most 0.015.
Values may be sent and summed in bfloat16 or wider, within the bound.
A program may use at most 64 MiB of HBM per device.

v0:
```python
import functools
import math

import jax
import jax.numpy as jnp
import ml_dtypes
import numpy as np
from jax import lax
from jax.experimental import pallas as pl
from jax.experimental.pallas import tpu as pltpu
from jax.sharding import PartitionSpec as P

MESH = pl.DeviceIdType.MESH
BF = jnp.bfloat16
F32 = jnp.float32
C = 32
HID = 128
XL = 8
YL = 16
NZ = 128
K2 = 2
NT = (((1,), (1,)), ((), ()))
NN = (((1,), (0,)), ((), ()))
TN = (((0,), (0,)), ((), ()))


def dot(a, b, dims):
    return lax.dot_general(a, b, dims, preferred_element_type=F32)


def signed(count, length):
    index = np.arange(count)
    return np.where(index < count // 2, index, index - count + length)


def angles(positions, freqs, length):
    return 2.0 * math.pi * ((positions[:, None] * freqs[None, :]) % length) / length


def tables(npx, npy, mx):
    nx, ny, my, mz = XL * npx, YL * npy, npx, K2 * npy
    ang = angles(np.arange(NZ), np.arange(mz), NZ)
    fwd = np.stack([np.cos(ang), -np.sin(ang)]) * 0.125
    fwd = fwd.reshape(2, NZ, npy, K2).transpose(2, 0, 3, 1)
    a1 = np.zeros((2, npy, 2, 4, K2, 2, NZ))
    for q in range(2):
        for c in range(2):
            a1[q, :, :, 2 * q + c, :, c, :] = fwd
    a1 = a1.reshape(2, npy * 16, 2 * NZ)
    ang = angles(np.arange(ny), signed(my, ny), ny)
    cs = np.stack([np.cos(ang), np.sin(ang)]).reshape(2, npy // 2, 2, YL, my)
    a2 = np.zeros((npy // 2, 2, my, XL, 2, XL, YL))
    for x in range(XL):
        a2[:, :, :, x, :, x, :] = cs.transpose(1, 0, 4, 2, 3)
    a2 = a2.reshape(npy // 2, 2 * my * XL, 2 * XL * YL)
    ang = angles(np.arange(nx), signed(mx, nx), nx)
    cs = np.stack([np.cos(ang), np.sin(ang)])
    tx = cs.transpose(0, 2, 1).reshape(2 * mx, nx) / math.sqrt(nx * ny)
    tix = cs.reshape(2 * nx, mx) / math.sqrt(mx * my)
    ang = angles(np.arange(NZ), np.arange(mz), NZ)
    weight = np.where(np.arange(mz) == 0, 1.0, 2.0) * (8.0 / math.sqrt(NZ * mz))
    inv = np.stack([np.cos(ang), -np.sin(ang)]) * weight
    inv = inv.reshape(2, NZ, npy, K2).transpose(2, 0, 3, 1)
    b7 = np.zeros((npy, 2, 8, K2, 8, NZ))
    for o in range(8):
        b7[:, :, o, :, o, :] = inv
    b7 = b7.reshape(npy * 32, 8 * NZ)
    e8 = np.zeros((2 * C, 8, 2 * C, K2))
    for r in range(8):
        e8[np.arange(2 * C), r, np.arange(2 * C), r % 2] = 1.0
    e8 = e8.reshape(2 * C * 8, 2 * C * K2)

    def half(t):
        return t.astype(np.float32).astype(ml_dtypes.bfloat16)

    def two(t):
        high = half(t)
        return np.stack([high, half(t - high.astype(np.float64))])

    return half(a1), half(a2), two(tx), two(tix), half(b7), half(e8)


def split(value):
    high = value.astype(BF)
    return high, (value - high.astype(F32)).astype(BF)


def dot3(table, value, dims):
    high, low = split(value)
    return dot(table[0], high, dims) + dot(table[0], low, dims) + dot(table[1], high, dims)


def gelu(v):
    k = math.sqrt(2.0 / math.pi)
    half = 0.5 * v
    return half + half * jnp.tanh(v * (k + (k * 0.044715) * (v * v)))


def kernel(
    npx, npy,
    f_ref, a1_ref, win_ref, bin_ref, wout_ref, w_hbm, a2_hbm, tx_hbm, tix_hbm, b7_hbm, e8_hbm,
    out_ref,
    zs, send1, recv1, send2, recv2, send3, recv3, send4, recv4,
    w_ref, a2_ref, tx_ref, tix_ref, b7_ref, e8_ref,
    k1, k2, bias, chan, xpat,
    ssem1, rsem1, ssem2, rsem2, ssem3, rsem3, ssem4, rsem4, tsem,
):
    ny = npy // 2
    mx = w_ref.shape[-1]
    mex = lax.axis_index("px")
    mey = lax.axis_index("py")
    my_chip = mey // 2
    my_core = mey % 2
    twin = my_chip * 2 + 1 - my_core

    loads = [
        pltpu.make_async_copy(src, dst, tsem.at[i])
        for i, (src, dst) in enumerate(
            [(a2_hbm, a2_ref), (tx_hbm, tx_ref), (e8_hbm, e8_ref), (w_hbm, w_ref), (tix_hbm, tix_ref), (b7_hbm, b7_ref)]
        )
    ]
    barrier = pltpu.get_barrier_semaphore()

    def greet_y(d, carry):
        pl.semaphore_signal(barrier, inc=1, device_id=(mex, lax.rem(mey + d, npy)), device_id_type=MESH)
        return carry

    def greet_x(d, carry):
        pl.semaphore_signal(barrier, inc=1, device_id=(lax.rem(mex + d, npx), mey), device_id_type=MESH)
        return carry

    lax.fori_loop(1, npy, greet_y, 0)
    lax.fori_loop(1, npx, greet_x, 0)
    for load in loads:
        load.start()

    def forward_z(g, carry):
        f4 = f_ref[pl.ds(g * 4, 4)]
        acc = dot(a1_ref[0], jnp.concatenate([f4[0], f4[1]], axis=1), NT)
        acc = acc + dot(a1_ref[1], jnp.concatenate([f4[2], f4[3]], axis=1), NT)
        zs[:, :, pl.ds(g, 1)] = acc.reshape(npy, 2, 1, 8, 128)
        return carry

    lax.fori_loop(0, C // 4, forward_z, 0, unroll=2)
    send1[...] = zs[...].reshape(npy, 128, 128).astype(BF)

    pl.semaphore_wait(barrier, npx + npy - 2)

    def y_copy(src, dst, ssem, rsem, target):
        return pltpu.make_async_remote_copy(
            src_ref=src.at[target], dst_ref=dst.at[mey], send_sem=ssem.at[target], recv_sem=rsem.at[mey],
            device_id=(mex, target), device_id_type=MESH,
        )

    def y_arrive(src, dst, ssem, rsem, source):
        pltpu.make_async_remote_copy(
            src_ref=src.at[source], dst_ref=dst.at[source], send_sem=ssem.at[source], recv_sem=rsem.at[source],
            device_id=(mex, source), device_id_type=MESH,
        ).wait_recv()

    def x_copy(src, dst, ssem, rsem, target):
        return pltpu.make_async_remote_copy(
            src_ref=src.at[target], dst_ref=dst.at[mex], send_sem=ssem.at[target], recv_sem=rsem.at[mex],
            device_id=(target, mey), device_id_type=MESH,
        )

    def x_exchange(src, dst, ssem, rsem):
        def start(d, carry):
            x_copy(src, dst, ssem, rsem, lax.rem(mex + d, npx)).start()
            return carry

        lax.fori_loop(1, npx, start, 0)
        dst[pl.ds(mex, 1)] = src[pl.ds(mex, 1)]

        def arrive(d, carry):
            source = lax.rem(mex + d, npx)
            pltpu.make_async_remote_copy(
                src_ref=src.at[source], dst_ref=dst.at[source], send_sem=ssem.at[source], recv_sem=rsem.at[source],
                device_id=(source, mey), device_id_type=MESH,
            ).wait_recv()
            return carry

        lax.fori_loop(1, npx, arrive, 0)

    def y_peers(far_first):
        offsets = sorted(range(1, ny), key=lambda d: min(d, ny - d), reverse=far_first)
        return [lax.rem(my_chip + d, ny) for d in offsets]

    for chip in y_peers(True):
        for core in range(2):
            y_copy(send1, recv1, ssem1, rsem1, chip * 2 + core).start()
    y_copy(send1, recv1, ssem1, rsem1, twin).start()
    recv1[pl.ds(mey, 1)] = send1[pl.ds(mey, 1)]

    spread = (lax.broadcasted_iota(jnp.int32, (C, C * 8), 1) // 8 == lax.broadcasted_iota(jnp.int32, (C, C * 8), 0))
    rows = dot(win_ref[...], spread.astype(F32).astype(BF), TN)
    same = lax.broadcasted_iota(jnp.int32, (HID, 8, C * 8), 1) == lax.rem(
        lax.broadcasted_iota(jnp.int32, (HID, 8, C * 8), 2), 8
    )
    k1[...] = jnp.where(same, rows[:, None, :], 0.0).reshape(HID * 8, C * 8).astype(BF)
    spread = (
        lax.broadcasted_iota(jnp.int32, (HID, HID * 8), 1) // 8 == lax.broadcasted_iota(jnp.int32, (HID, HID * 8), 0)
    )
    rows = dot(wout_ref[...], spread.astype(F32).astype(BF), NN)
    same = lax.broadcasted_iota(jnp.int32, (C, 8, HID * 8), 1) == lax.rem(
        lax.broadcasted_iota(jnp.int32, (C, 8, HID * 8), 2), 8
    )
    k2[...] = jnp.where(same, rows[:, None, :], 0.0).reshape(C * 8, HID * 8).astype(BF)
    turned = jnp.transpose(jnp.broadcast_to(bin_ref[...], (HID, HID)))
    bias[...] = jnp.broadcast_to(turned[:, None, :], (HID, 8, 128)).reshape(HID * 8, 128)

    def channel(i, carry):
        block = f_ref[:, pl.ds(pl.multiple_of(i * 16, 16), 16), :].astype(F32)
        cells = jnp.concatenate(
            [block[:, :8].reshape(C * 8, 128), block[:, 8:].reshape(C * 8, 128)], axis=1
        ).astype(BF)
        acc = jnp.zeros((C * 8, 256), F32)
        for part in range(4):
            rows = slice(part * 256, part * 256 + 256)
            b = bias[rows]
            hidden = gelu(dot(k1[rows], cells, NN) + jnp.concatenate([b, b], axis=1)).astype(BF)
            acc = acc + dot(k2[:, rows], hidden, NN)
        chan[:, pl.ds(pl.multiple_of(i * 16, 16), 8), :] = acc[:, :128].reshape(C, 8, 128)
        chan[:, pl.ds(pl.multiple_of(i * 16 + 8, 8), 8), :] = acc[:, 128:].reshape(C, 8, 128)
        return carry

    lax.fori_loop(0, 4, channel, 0)

    loads[0].wait()
    lane = lax.broadcasted_iota(jnp.int32, (1, 128), 1)
    sign = jnp.where(lane < 64, 1.0, -1.0)

    def y_part(chip):
        pair = jnp.concatenate([recv1[chip * 2], recv1[chip * 2 + 1]], axis=1)
        return dot(a2_ref[chip], pair, NT)

    y_arrive(send1, recv1, ssem1, rsem1, twin)
    acc = y_part(my_chip)
    for chip in y_peers(False):
        for core in range(2):
            y_arrive(send1, recv1, ssem1, rsem1, chip * 2 + core)
        acc = acc + y_part(chip)
    half = npx * XL
    lines = acc[:half] + sign * pltpu.roll(acc[half:], 64, 1)
    send2[...] = lines.reshape(npx, XL, 128).astype(BF)
    x_exchange(send2, recv2, ssem2, rsem2)

    loads[1].wait()
    loads[2].wait()
    block = recv2[...].astype(F32).reshape(half, 128).astype(BF)
    both = dot(tx_ref[0], block, NN) + dot(tx_ref[1], block, NN)
    spectra = both[:mx] + sign * pltpu.roll(both[mx:], 64, 1)
    high, low = split(spectra)
    xpat[...] = (dot(e8_ref[...], high, NT) + dot(e8_ref[...], low, NT)).reshape(2 * C, 8, mx)

    loads[3].wait()

    def mix(c, carry):
        real, imag = carry
        wr = w_ref[0, c].astype(F32).reshape(8, 8, mx)
        wi = w_ref[1, c].astype(F32).reshape(8, 8, mx)
        xr = xpat[c][None]
        xi = xpat[c + C][None]
        return real + xr * wr - xi * wi, imag + xr * wi + xi * wr

    zero = jnp.zeros((8, 8, mx), F32)
    real, imag = lax.fori_loop(0, C, mix, (zero, zero), unroll=4)
    modes = jnp.concatenate([real.reshape(64, mx), imag.reshape(64, mx)], axis=0)

    loads[4].wait()
    both = dot3(tix_ref, modes, NT)
    cells = both[:half] - sign * pltpu.roll(both[half:], 64, 1)
    send3[...] = cells.reshape(npx, XL, 128).astype(BF)
    x_exchange(send3, recv3, ssem3, rsem3)

    block = recv3[...].astype(F32).reshape(half, 128)
    turned = jnp.concatenate([block, -sign * pltpu.roll(block, 64, 1)], axis=0)
    turned = jnp.transpose(turned).astype(BF)

    def y_back(chip):
        both = dot(turned, a2_ref[chip], NN).astype(BF)
        send4[pl.ds(chip * 2, 1)] = both[:, :128][None]
        send4[pl.ds(chip * 2 + 1, 1)] = both[:, 128:][None]

    for chip in y_peers(True):
        y_back(chip)
        for core in range(2):
            y_copy(send4, recv4, ssem4, rsem4, chip * 2 + core).start()
    y_back(my_chip)
    y_copy(send4, recv4, ssem4, rsem4, twin).start()
    recv4[pl.ds(mey, 1)] = send4[pl.ds(mey, 1)]

    lax.fori_loop(4, 8, channel, 0)

    y_arrive(send4, recv4, ssem4, rsem4, twin)
    for chip in y_peers(False):
        for core in range(2):
            y_arrive(send4, recv4, ssem4, rsem4, chip * 2 + core)

    loads[5].wait()
    for g in range(4):
        lines = jnp.concatenate(
            [recv4[:, 16 * g : 16 * g + 16, :].reshape(npy, 1, 16, 128),
             recv4[:, 64 + 16 * g : 80 + 16 * g, :].reshape(npy, 1, 16, 128)], axis=1
        ).reshape(npy * 32, 128)
        values = dot(lines, b7_ref[...], TN)
        for o in range(8):
            total = values[:, 128 * o : 128 * o + 128] + chan[8 * g + o]
            out_ref[8 * g + o] = gelu(total).astype(BF)

    def sent_y(d, carry):
        target = lax.rem(mey + d, npy)
        y_copy(send1, recv1, ssem1, rsem1, target).wait_send()
        y_copy(send4, recv4, ssem4, rsem4, target).wait_send()
        return carry

    def sent_x(d, carry):
        target = lax.rem(mex + d, npx)
        x_copy(send2, recv2, ssem2, rsem2, target).wait_send()
        x_copy(send3, recv3, ssem3, rsem3, target).wait_send()
        return carry

    lax.fori_loop(1, npy, sent_y, 0)
    lax.fori_loop(1, npx, sent_x, 0)


def body(npx, npy, field, spec_weight, w_in, b_in, w_out):
    mx = spec_weight.shape[4]
    a1, a2, tx, tix, b7, e8 = tables(npx, npy, mx)
    cells = field.reshape(C, XL * YL, NZ)
    weight = jnp.transpose(spec_weight[0], (0, 1, 2, 4, 5, 3)).reshape(2, C, C * K2, mx)
    vmem = pl.BlockSpec(memory_space=pltpu.VMEM)
    anywhere = pl.BlockSpec(memory_space=pl.ANY)
    out = pl.pallas_call(
        functools.partial(kernel, npx, npy),
        out_shape=jax.ShapeDtypeStruct((C, XL * YL, NZ), BF),
        in_specs=[vmem] * 5 + [anywhere] * 6,
        out_specs=vmem,
        scratch_shapes=[
            pltpu.VMEM((npy, 2, 8, 8, 128), F32),
            pltpu.VMEM((npy, 128, 128), BF),
            pltpu.VMEM((npy, 128, 128), BF),
            pltpu.VMEM((npx, XL, 128), BF),
            pltpu.VMEM((npx, XL, 128), BF),
            pltpu.VMEM((npx, XL, 128), BF),
            pltpu.VMEM((npx, XL, 128), BF),
            pltpu.VMEM((npy, 128, 128), BF),
            pltpu.VMEM((npy, 128, 128), BF),
            pltpu.VMEM(weight.shape, BF),
            pltpu.VMEM(a2.shape, BF),
            pltpu.VMEM(tx.shape, BF),
            pltpu.VMEM(tix.shape, BF),
            pltpu.VMEM(b7.shape, BF),
            pltpu.VMEM(e8.shape, BF),
            pltpu.VMEM((HID * 8, C * 8), BF),
            pltpu.VMEM((C * 8, HID * 8), BF),
            pltpu.VMEM((HID * 8, 128), F32),
            pltpu.VMEM((C, XL * YL, NZ), F32),
            pltpu.VMEM((2 * C, 8, mx), F32),
            pltpu.SemaphoreType.DMA((npy,)),
            pltpu.SemaphoreType.DMA((npy,)),
            pltpu.SemaphoreType.DMA((npx,)),
            pltpu.SemaphoreType.DMA((npx,)),
            pltpu.SemaphoreType.DMA((npx,)),
            pltpu.SemaphoreType.DMA((npx,)),
            pltpu.SemaphoreType.DMA((npy,)),
            pltpu.SemaphoreType.DMA((npy,)),
            pltpu.SemaphoreType.DMA((6,)),
        ],
        compiler_params=pltpu.CompilerParams(
            collective_id=0, has_side_effects=True, vmem_limit_bytes=60 * 1024 * 1024
        ),
    )(
        cells, jnp.asarray(a1), w_in[0], b_in, jnp.transpose(w_out[0]), weight,
        jnp.asarray(a2), jnp.asarray(tx), jnp.asarray(tix), jnp.asarray(b7), jnp.asarray(e8),
    )
    return out.reshape(field.shape)


def solution(mesh):
    in_specs = (
        P(None, "px", "py", None),
        P(None, None, None, None, None, "px", "py"),
        P(),
        P(),
        P(),
    )
    return jax.shard_map(
        functools.partial(body, mesh.shape["px"], mesh.shape["py"]),
        mesh=mesh, in_specs=in_specs, out_specs=P(None, "px", "py", None), check_vma=False,
    )
```

profile of v0, /device:TPU:1, one launch (start us, length us, event | category | flops | bytes accessed | tf_op | source)
XLA Modules:
  0.0 64.9 jit_solution(5853622481961668802)
XLA Ops:
  0.0 62.4 %shard_map.109 = bf16[32,128,128]{2,1,0:T(8,128)(2,1)} custom-call(bf16[32,128,128]{2,1,0:T(8,128)(2,1)} %bitcast.12, bf16[2,256,256]{2,1,0:T(8,128)(2,1)} %constant.12.clone.a1_ref, bf16[32,128]{1,0:T(8,128)(2,1)} %bitcast.14, f32[1,128]{1,0:T(1,128)} %bin_ref.1, bf16[32,128]{1,0:T(8,128)(2,1)} %bitcast.15, bf16[2,32,64,32]{3,2,1,0:T(8,128)(2,1)} %bitcast.13, ...), custom_call_target="tpu_custom_call" | custom-call | tf_op jit(solution)/shard_map/pallas_call | solution.py:334
  62.4 2.5 %copy.13 = bf16[32,8,16,128]{3,2,1,0:T(8,128)(2,1)} copy(bf16[32,8,16,128]{3,2,1,0:T(8,128)(2,1)} %bitcast.11) | data formatting | bytes 2097152
where the time goes:
time: 65.1 us; the launch traced here: 64.9 us
  Pallas kernels  62.4 us (96%)
  local copies, waits for them, and re-layouts  2.49 us (4%)
    pallas_call x1, Pallas kernels, body(): pl.pallas_call(functools.partial(kernel, npx, npy), out_shape=jax.ShapeDt...  62.4 us
    unnamed x1, local copies, waits for them, and re-layouts  2.49 us

commit v1 on v0

--- a/solution.py
+++ b/solution.py
@@ -52,6 +52,7 @@
     a2 = np.zeros((npy // 2, 2, my, XL, 2, XL, YL))
     for x in range(XL):
         a2[:, :, :, x, :, x, :] = cs.transpose(1, 0, 4, 2, 3)
+    a2b = a2.transpose(0, 4, 2, 3, 1, 5, 6).reshape(npy, my * XL, 2 * XL * YL)
     a2 = a2.reshape(npy // 2, 2 * my * XL, 2 * XL * YL)
     ang = angles(np.arange(nx), signed(mx, nx), nx)
     cs = np.stack([np.cos(ang), np.sin(ang)])
@@ -77,7 +78,7 @@
         high = half(t)
         return np.stack([high, half(t - high.astype(np.float64))])
 
-    return half(a1), half(a2), two(tx), two(tix), half(b7), half(e8)
+    return half(a1), half(a2), half(a2b), two(tx), two(tix), half(b7), half(e8)
 
 
 def split(value):
@@ -98,12 +99,12 @@
 
 def kernel(
     npx, npy,
-    f_ref, a1_ref, win_ref, bin_ref, wout_ref, w_hbm, a2_hbm, tx_hbm, tix_hbm, b7_hbm, e8_hbm,
+    f_ref, a1_ref, win_ref, bin_ref, wout_ref, w_hbm, a2_hbm, a2b_hbm, tx_hbm, tix_hbm, b7_hbm, e8_hbm,
     out_ref,
-    zs, send1, recv1, send2, recv2, send3, recv3, send4, recv4,
-    w_ref, a2_ref, tx_ref, tix_ref, b7_ref, e8_ref,
+    zs, send1, recv1, send2, recv2, send3, recv3, ring, lines_y,
+    w_ref, a2_ref, a2b_ref, tx_ref, tix_ref, b7_ref, e8_ref,
     k1, k2, bias, chan, xpat,
-    ssem1, rsem1, ssem2, rsem2, ssem3, rsem3, ssem4, rsem4, tsem,
+    ssem1, rsem1, ssem2, rsem2, ssem3, rsem3, ring_on, ring_back, ring_twin, ring_in, tsem,
 ):
     ny = npy // 2
     mx = w_ref.shape[-1]
@@ -116,7 +117,8 @@
     loads = [
         pltpu.make_async_copy(src, dst, tsem.at[i])
         for i, (src, dst) in enumerate(
-            [(a2_hbm, a2_ref), (tx_hbm, tx_ref), (e8_hbm, e8_ref), (w_hbm, w_ref), (tix_hbm, tix_ref), (b7_hbm, b7_ref)]
+            [(a2_hbm, a2_ref), (tx_hbm, tx_ref), (e8_hbm, e8_ref), (w_hbm, w_ref), (tix_hbm, tix_ref), (b7_hbm, b7_ref),
+             (a2b_hbm.at[mey], a2b_ref)]
         )
     ]
     barrier = pltpu.get_barrier_semaphore()
@@ -164,13 +166,14 @@
             device_id=(target, mey), device_id_type=MESH,
         )
 
-    def x_exchange(src, dst, ssem, rsem):
+    def x_exchange(src, dst, ssem, rsem, meanwhile):
         def start(d, carry):
             x_copy(src, dst, ssem, rsem, lax.rem(mex + d, npx)).start()
             return carry
 
         lax.fori_loop(1, npx, start, 0)
         dst[pl.ds(mex, 1)] = src[pl.ds(mex, 1)]
+        channel(meanwhile, 0)
 
         def arrive(d, carry):
             source = lax.rem(mex + d, npx)
@@ -224,7 +227,7 @@
         chan[:, pl.ds(pl.multiple_of(i * 16 + 8, 8), 8), :] = acc[:, 128:].reshape(C, 8, 128)
         return carry
 
-    lax.fori_loop(0, 4, channel, 0)
+    lax.fori_loop(0, 2, channel, 0)
 
     loads[0].wait()
     lane = lax.broadcasted_iota(jnp.int32, (1, 128), 1)
@@ -243,7 +246,7 @@
     half = npx * XL
     lines = acc[:half] + sign * pltpu.roll(acc[half:], 64, 1)
     send2[...] = lines.reshape(npx, XL, 128).astype(BF)
-    x_exchange(send2, recv2, ssem2, rsem2)
+    x_exchange(send2, recv2, ssem2, rsem2, 2)
 
     loads[1].wait()
     loads[2].wait()
@@ -271,37 +274,72 @@
     both = dot3(tix_ref, modes, NT)
     cells = both[:half] - sign * pltpu.roll(both[half:], 64, 1)
     send3[...] = cells.reshape(npx, XL, 128).astype(BF)
-    x_exchange(send3, recv3, ssem3, rsem3)
-
-    block = recv3[...].astype(F32).reshape(half, 128)
-    turned = jnp.concatenate([block, -sign * pltpu.roll(block, 64, 1)], axis=0)
-    turned = jnp.transpose(turned).astype(BF)
-
-    def y_back(chip):
-        both = dot(turned, a2_ref[chip], NN).astype(BF)
-        send4[pl.ds(chip * 2, 1)] = both[:, :128][None]
-        send4[pl.ds(chip * 2 + 1, 1)] = both[:, 128:][None]
-
-    for chip in y_peers(True):
-        y_back(chip)
-        for core in range(2):
-            y_copy(send4, recv4, ssem4, rsem4, chip * 2 + core).start()
-    y_back(my_chip)
-    y_copy(send4, recv4, ssem4, rsem4, twin).start()
-    recv4[pl.ds(mey, 1)] = send4[pl.ds(mey, 1)]
-
-    lax.fori_loop(4, 8, channel, 0)
-
-    y_arrive(send4, recv4, ssem4, rsem4, twin)
-    for chip in y_peers(False):
-        for core in range(2):
-            y_arrive(send4, recv4, ssem4, rsem4, chip * 2 + core)
+    x_exchange(send3, recv3, ssem3, rsem3, 3)
+
+    block = jnp.transpose(recv3[...].astype(F32).reshape(half, 128)).astype(BF)
+    ring[pl.ds(mey, 1)] = block.reshape(1, 2, 64, half)
+    right = lax.rem(my_chip + 1, ny) * 2 + my_core
+    left = lax.rem(my_chip + ny - 1, ny) * 2 + my_core
+
+    def ring_copy(p, q, sem, target):
+        return pltpu.make_async_remote_copy(
+            src_ref=ring.at[p, q], dst_ref=ring.at[p, q], send_sem=sem.at[p, q], recv_sem=ring_in.at[p, q],
+            device_id=(mex, target), device_id_type=MESH,
+        )
+
+    def cells_back(p):
+        both = dot(ring[p].reshape(128, half), a2b_ref[...], NN)
+        real = both[:64, :128] - both[64:, 128:]
+        imag = both[64:, :128] + both[:64, 128:]
+        lines_y[pl.ds(p, 1)] = jnp.concatenate([real, imag], axis=0).astype(BF)[None]
+
+    reach = {("right", 0): ny // 2, ("left", 1): ny // 2, ("right", 1): (ny - 1) // 2, ("left", 0): (ny - 1) // 2}
+    order = [("right", 0), ("left", 1), ("right", 1), ("left", 0)]
+    sends = []
+
+    def go(p, q, sem, target):
+        copy = ring_copy(p, q, sem, target)
+        copy.start()
+        sends.append(copy)
+
+    for way, q in order:
+        if reach[way, q] >= 1:
+            go(mey, q, ring_on if way == "right" else ring_back, right if way == "right" else left)
+    for q in range(2):
+        go(mey, q, ring_twin, twin)
+    loads[6].wait()
+    cells_back(mey)
+    done = 4
+    for k in range(1, ny // 2 + 1):
+        behind = lax.rem(my_chip + ny - k, ny) * 2
+        ahead = lax.rem(my_chip + k, ny) * 2
+        for way, q in order:
+            if k <= reach[way, q]:
+                p = (behind if way == "right" else ahead) + my_core
+                ring_copy(p, q, ring_on, twin).wait_recv()
+                if k < reach[way, q]:
+                    go(p, q, ring_on, right if way == "right" else left)
+                go(p, q, ring_twin, twin)
+        if done < 8:
+            channel(done, 0)
+            done += 1
+        cells_back(behind + my_core)
+        if 2 * k < ny:
+            cells_back(ahead + my_core)
+    for more in range(done, 8):
+        channel(more, 0)
+    for k in range(ny // 2 + 1):
+        for p in sorted({k, (ny - k) % ny}):
+            p = lax.rem(my_chip + p, ny) * 2 + 1 - my_core
+            for q in range(2):
+                ring_copy(p, q, ring_on, twin).wait_recv()
+            cells_back(p)
 
     loads[5].wait()
     for g in range(4):
         lines = jnp.concatenate(
-            [recv4[:, 16 * g : 16 * g + 16, :].reshape(npy, 1, 16, 128),
-             recv4[:, 64 + 16 * g : 80 + 16 * g, :].reshape(npy, 1, 16, 128)], axis=1
+            [lines_y[:, 16 * g : 16 * g + 16, :].reshape(npy, 1, 16, 128),
+             lines_y[:, 64 + 16 * g : 80 + 16 * g, :].reshape(npy, 1, 16, 128)], axis=1
         ).reshape(npy * 32, 128)
         values = dot(lines, b7_ref[...], TN)
         for o in range(8):
@@ -311,7 +349,6 @@
     def sent_y(d, carry):
         target = lax.rem(mey + d, npy)
         y_copy(send1, recv1, ssem1, rsem1, target).wait_send()
-        y_copy(send4, recv4, ssem4, rsem4, target).wait_send()
         return carry
 
     def sent_x(d, carry):
@@ -322,11 +359,13 @@
 
     lax.fori_loop(1, npy, sent_y, 0)
     lax.fori_loop(1, npx, sent_x, 0)
+    for copy in sends:
+        copy.wait_send()
 
 
 def body(npx, npy, field, spec_weight, w_in, b_in, w_out):
     mx = spec_weight.shape[4]
-    a1, a2, tx, tix, b7, e8 = tables(npx, npy, mx)
+    a1, a2, a2b, tx, tix, b7, e8 = tables(npx, npy, mx)
     cells = field.reshape(C, XL * YL, NZ)
     weight = jnp.transpose(spec_weight[0], (0, 1, 2, 4, 5, 3)).reshape(2, C, C * K2, mx)
     vmem = pl.BlockSpec(memory_space=pltpu.VMEM)
@@ -334,7 +373,7 @@
     out = pl.pallas_call(
         functools.partial(kernel, npx, npy),
         out_shape=jax.ShapeDtypeStruct((C, XL * YL, NZ), BF),
-        in_specs=[vmem] * 5 + [anywhere] * 6,
+        in_specs=[vmem] * 5 + [anywhere] * 7,
         out_specs=vmem,
         scratch_shapes=[
             pltpu.VMEM((npy, 2, 8, 8, 128), F32),
@@ -344,10 +383,11 @@
             pltpu.VMEM((npx, XL, 128), BF),
             pltpu.VMEM((npx, XL, 128), BF),
             pltpu.VMEM((npx, XL, 128), BF),
-            pltpu.VMEM((npy, 128, 128), BF),
+            pltpu.VMEM((npy, 2, 64, npx * XL), BF),
             pltpu.VMEM((npy, 128, 128), BF),
             pltpu.VMEM(weight.shape, BF),
             pltpu.VMEM(a2.shape, BF),
+            pltpu.VMEM(a2b.shape[1:], BF),
             pltpu.VMEM(tx.shape, BF),
             pltpu.VMEM(tix.shape, BF),
             pltpu.VMEM(b7.shape, BF),
@@ -363,16 +403,18 @@
             pltpu.SemaphoreType.DMA((npx,)),
             pltpu.SemaphoreType.DMA((npx,)),
             pltpu.SemaphoreType.DMA((npx,)),
-            pltpu.SemaphoreType.DMA((npy,)),
-            pltpu.SemaphoreType.DMA((npy,)),
-            pltpu.SemaphoreType.DMA((6,)),
+            pltpu.SemaphoreType.DMA((npy, 2)),
+            pltpu.SemaphoreType.DMA((npy, 2)),
+            pltpu.SemaphoreType.DMA((npy, 2)),
+            pltpu.SemaphoreType.DMA((npy, 2)),
+            pltpu.SemaphoreType.DMA((7,)),
         ],
         compiler_params=pltpu.CompilerParams(
             collective_id=0, has_side_effects=True, vmem_limit_bytes=60 * 1024 * 1024
         ),
     )(
         cells, jnp.asarray(a1), w_in[0], b_in, jnp.transpose(w_out[0]), weight,
-        jnp.asarray(a2), jnp.asarray(tx), jnp.asarray(tix), jnp.asarray(b7), jnp.asarray(e8),
+        jnp.asarray(a2), jnp.asarray(a2b), jnp.asarray(tx), jnp.asarray(tix), jnp.asarray(b7), jnp.asarray(e8),
     )
     return out.reshape(field.shape)
 

time: 65.1 us -> 68.1 us (1.046)
  Pallas kernels: 62.4 us -> 64.7 us
    pallas_call x1, Pallas kernels: 62.4 us -> 64.7 us  [body(): pl.pallas_call(functools.partial(kernel, npx, npy), out_shape=jax.ShapeDt...]
where the time goes in v1:
time: 68.1 us; the launch traced here: 67.2 us
  Pallas kernels  64.7 us (95%)
  local copies, waits for them, and re-layouts  2.49 us (4%)
    pallas_call x1, Pallas kernels, body(): pl.pallas_call(functools.partial(kernel, npx, npy), out_shape=jax.ShapeDt...  64.7 us
    unnamed x1, local copies, waits for them, and re-layouts  2.49 us

profile of v1, /device:TPU:1, one launch (start us, length us, event | category | flops | bytes accessed | tf_op | source)
XLA Modules:
  0.0 67.2 jit_solution(10514924352837269758)
XLA Ops:
  0.0 64.7 %shard_map.118 = bf16[32,128,128]{2,1,0:T(8,128)(2,1)} custom-call(bf16[32,128,128]{2,1,0:T(8,128)(2,1)} %bitcast.12, bf16[2,256,256]{2,1,0:T(8,128)(2,1)} %constant.14.clone.a1_ref, bf16[32,128]{1,0:T(8,128)(2,1)} %bitcast.14, f32[1,128]{1,0:T(1,128)} %bin_ref.1, bf16[32,128]{1,0:T(8,128)(2,1)} %bitcast.15, bf16[2,32,64,32]{3,2,1,0:T(8,128)(2,1)} %bitcast.13, ...), custom_call_target="tpu_custom_call" | custom-call | tf_op jit(solution)/shard_map/pallas_call | solution.py:373
  64.7 2.5 %copy.14 = bf16[32,8,16,128]{3,2,1,0:T(8,128)(2,1)} copy(bf16[32,8,16,128]{3,2,1,0:T(8,128)(2,1)} %bitcast.11) | data formatting | bytes 2097152

commit v2 on v0

--- a/solution.py
+++ b/solution.py
@@ -22,6 +22,11 @@
 NT = (((1,), (1,)), ((), ()))
 NN = (((1,), (0,)), ((), ()))
 TN = (((0,), (0,)), ((), ()))
+
+
+def chips(npx):
+    zc = max(npx // 4, min(npx, 2))
+    return npx // zc, zc
 
 
 def dot(a, b, dims):
@@ -98,41 +103,51 @@
 
 def kernel(
     npx, npy,
-    f_ref, a1_ref, win_ref, bin_ref, wout_ref, w_hbm, a2_hbm, tx_hbm, tix_hbm, b7_hbm, e8_hbm,
-    out_ref,
-    zs, send1, recv1, send2, recv2, send3, recv3, send4, recv4,
-    w_ref, a2_ref, tx_ref, tix_ref, b7_ref, e8_ref,
-    k1, k2, bias, chan, xpat,
-    ssem1, rsem1, ssem2, rsem2, ssem3, rsem3, ssem4, rsem4, tsem,
+    f_hbm, a1_hbm, win_hbm, bin_hbm, wout_hbm, w_hbm, a2_hbm, tx_hbm, tix_hbm, e8_hbm,
+    recv4, chan,
+    zs, send1, recv1, send2, mid2, recv2, send3, mid3, recv3, send4,
+    f_ref, a1_ref, win_ref, bin_ref, wout_ref, w_ref, a2_ref, tx_ref, tix_ref, e8_ref,
+    k1, k2, bias, xpat,
+    ssem1, rsem1, sems2, sems3, ssem4, rsem4, tsem,
 ):
     ny = npy // 2
     mx = w_ref.shape[-1]
+    xc, zc = chips(npx)
+    sent = []
     mex = lax.axis_index("px")
     mey = lax.axis_index("py")
     my_chip = mey // 2
     my_core = mey % 2
     twin = my_chip * 2 + 1 - my_core
-
-    loads = [
-        pltpu.make_async_copy(src, dst, tsem.at[i])
-        for i, (src, dst) in enumerate(
-            [(a2_hbm, a2_ref), (tx_hbm, tx_ref), (e8_hbm, e8_ref), (w_hbm, w_ref), (tix_hbm, tix_ref), (b7_hbm, b7_ref)]
-        )
+    mex_x = mex // zc
+    mex_z = mex % zc
+
+    def load(i, src, dst):
+        return pltpu.make_async_copy(src, dst, tsem.at[i])
+
+    cells_in = [load(0, a1_hbm, a1_ref)] + [
+        load(1 + i, f_hbm.at[pl.ds(i * 8, 8)], f_ref.at[pl.ds(i * 8, 8)]) for i in range(4)
     ]
+    pairs = [(win_hbm, win_ref), (bin_hbm, bin_ref), (wout_hbm, wout_ref), (a2_hbm, a2_ref), (tx_hbm, tx_ref),
+             (e8_hbm, e8_ref), (w_hbm, w_ref), (tix_hbm, tix_ref)]
+    loads = [load(5 + i, src, dst) for i, (src, dst) in enumerate(pairs)]
     barrier = pltpu.get_barrier_semaphore()
 
     def greet_y(d, carry):
         pl.semaphore_signal(barrier, inc=1, device_id=(mex, lax.rem(mey + d, npy)), device_id_type=MESH)
         return carry
 
-    def greet_x(d, carry):
-        pl.semaphore_signal(barrier, inc=1, device_id=(lax.rem(mex + d, npx), mey), device_id_type=MESH)
-        return carry
-
+    for load in cells_in + loads:
+        load.start()
     lax.fori_loop(1, npy, greet_y, 0)
-    lax.fori_loop(1, npx, greet_x, 0)
-    for load in loads:
-        load.start()
+    for d in range(1, zc):
+        pl.semaphore_signal(
+            barrier, inc=1, device_id=(mex_x * zc + lax.rem(mex_z + d, zc), mey), device_id_type=MESH
+        )
+    for d in range(1, xc):
+        pl.semaphore_signal(
+            barrier, inc=1, device_id=(lax.rem(mex_x + d, xc) * zc + mex_z, mey), device_id_type=MESH
+        )
 
     def forward_z(g, carry):
         f4 = f_ref[pl.ds(g * 4, 4)]
@@ -141,10 +156,13 @@
         zs[:, :, pl.ds(g, 1)] = acc.reshape(npy, 2, 1, 8, 128)
         return carry
 
-    lax.fori_loop(0, C // 4, forward_z, 0, unroll=2)
+    cells_in[0].wait()
+    for i in range(4):
+        cells_in[1 + i].wait()
+        lax.fori_loop(2 * i, 2 * i + 2, forward_z, 0, unroll=2)
     send1[...] = zs[...].reshape(npy, 128, 128).astype(BF)
 
-    pl.semaphore_wait(barrier, npx + npy - 2)
+    pl.semaphore_wait(barrier, npy + zc + xc - 3)
 
     def y_copy(src, dst, ssem, rsem, target):
         return pltpu.make_async_remote_copy(
@@ -158,29 +176,30 @@
             device_id=(mex, source), device_id_type=MESH,
         ).wait_recv()
 
-    def x_copy(src, dst, ssem, rsem, target):
-        return pltpu.make_async_remote_copy(
-            src_ref=src.at[target], dst_ref=dst.at[mex], send_sem=ssem.at[target], recv_sem=rsem.at[mex],
-            device_id=(target, mey), device_id_type=MESH,
-        )
-
-    def x_exchange(src, dst, ssem, rsem):
-        def start(d, carry):
-            x_copy(src, dst, ssem, rsem, lax.rem(mex + d, npx)).start()
-            return carry
-
-        lax.fori_loop(1, npx, start, 0)
-        dst[pl.ds(mex, 1)] = src[pl.ds(mex, 1)]
-
-        def arrive(d, carry):
-            source = lax.rem(mex + d, npx)
-            pltpu.make_async_remote_copy(
-                src_ref=src.at[source], dst_ref=dst.at[source], send_sem=ssem.at[source], recv_sem=rsem.at[source],
-                device_id=(source, mey), device_id_type=MESH,
-            ).wait_recv()
-            return carry
-
-        lax.fori_loop(1, npx, arrive, 0)
+    def x_exchange(src, mid, dst, sems):
+        def hop(first, target, slot):
+            if first:
+                return pltpu.make_async_remote_copy(
+                    src_ref=src.at[:, target], dst_ref=mid.at[:, slot], send_sem=sems.at[0, target],
+                    recv_sem=sems.at[1, slot], device_id=(mex_x * zc + target, mey), device_id_type=MESH,
+                )
+            return pltpu.make_async_remote_copy(
+                src_ref=mid.at[target], dst_ref=dst.at[slot], send_sem=sems.at[2, target],
+                recv_sem=sems.at[3, slot], device_id=(target * zc + mex_z, mey), device_id_type=MESH,
+            )
+
+        for first, own, count in ((True, mex_z, zc), (False, mex_x, xc)):
+            others = [lax.rem(own + d, count) for d in sorted(range(1, count), key=lambda d: -min(d, count - d))]
+            for other in others:
+                hop(first, other, own).start()
+            if first:
+                mid[:, pl.ds(own, 1)] = src[:, pl.ds(own, 1)]
+            else:
+                dst[pl.ds(own, 1)] = mid[pl.ds(own, 1)]
+            for other in others:
+                hop(first, other, other).wait_recv()
+            for other in others:
+                sent.append(hop(first, other, own))
 
     def y_peers(far_first):
         offsets = sorted(range(1, ny), key=lambda d: min(d, ny - d), reverse=far_first)
@@ -192,18 +211,20 @@
     y_copy(send1, recv1, ssem1, rsem1, twin).start()
     recv1[pl.ds(mey, 1)] = send1[pl.ds(mey, 1)]
 
-    spread = (lax.broadcasted_iota(jnp.int32, (C, C * 8), 1) // 8 == lax.broadcasted_iota(jnp.int32, (C, C * 8), 0))
+    for i in range(3):
+        loads[i].wait()
+    spread = (lax.broadcasted_iota(jnp.int32, (C, C * 8), 1) >> 3 == lax.broadcasted_iota(jnp.int32, (C, C * 8), 0))
     rows = dot(win_ref[...], spread.astype(F32).astype(BF), TN)
-    same = lax.broadcasted_iota(jnp.int32, (HID, 8, C * 8), 1) == lax.rem(
-        lax.broadcasted_iota(jnp.int32, (HID, 8, C * 8), 2), 8
+    same = lax.broadcasted_iota(jnp.int32, (HID, 8, C * 8), 1) == (
+        lax.broadcasted_iota(jnp.int32, (HID, 8, C * 8), 2) & 7
     )
     k1[...] = jnp.where(same, rows[:, None, :], 0.0).reshape(HID * 8, C * 8).astype(BF)
     spread = (
-        lax.broadcasted_iota(jnp.int32, (HID, HID * 8), 1) // 8 == lax.broadcasted_iota(jnp.int32, (HID, HID * 8), 0)
+        lax.broadcasted_iota(jnp.int32, (HID, HID * 8), 1) >> 3 == lax.broadcasted_iota(jnp.int32, (HID, HID * 8), 0)
     )
     rows = dot(wout_ref[...], spread.astype(F32).astype(BF), NN)
-    same = lax.broadcasted_iota(jnp.int32, (C, 8, HID * 8), 1) == lax.rem(
-        lax.broadcasted_iota(jnp.int32, (C, 8, HID * 8), 2), 8
+    same = lax.broadcasted_iota(jnp.int32, (C, 8, HID * 8), 1) == (
+        lax.broadcasted_iota(jnp.int32, (C, 8, HID * 8), 2) & 7
     )
     k2[...] = jnp.where(same, rows[:, None, :], 0.0).reshape(C * 8, HID * 8).astype(BF)
     turned = jnp.transpose(jnp.broadcast_to(bin_ref[...], (HID, HID)))
@@ -226,7 +247,7 @@
 
     lax.fori_loop(0, 4, channel, 0)
 
-    loads[0].wait()
+    loads[3].wait()
     lane = lax.broadcasted_iota(jnp.int32, (1, 128), 1)
     sign = jnp.where(lane < 64, 1.0, -1.0)
 
@@ -242,18 +263,18 @@
         acc = acc + y_part(chip)
     half = npx * XL
     lines = acc[:half] + sign * pltpu.roll(acc[half:], 64, 1)
-    send2[...] = lines.reshape(npx, XL, 128).astype(BF)
-    x_exchange(send2, recv2, ssem2, rsem2)
-
-    loads[1].wait()
-    loads[2].wait()
+    send2[...] = lines.reshape(xc, zc, XL, 128).astype(BF)
+    x_exchange(send2, mid2, recv2, sems2)
+
+    loads[4].wait()
+    loads[5].wait()
     block = recv2[...].astype(F32).reshape(half, 128).astype(BF)
     both = dot(tx_ref[0], block, NN) + dot(tx_ref[1], block, NN)
     spectra = both[:mx] + sign * pltpu.roll(both[mx:], 64, 1)
     high, low = split(spectra)
     xpat[...] = (dot(e8_ref[...], high, NT) + dot(e8_ref[...], low, NT)).reshape(2 * C, 8, mx)
 
-    loads[3].wait()
+    loads[6].wait()
 
     def mix(c, carry):
         real, imag = carry
@@ -267,11 +288,11 @@
     real, imag = lax.fori_loop(0, C, mix, (zero, zero), unroll=4)
     modes = jnp.concatenate([real.reshape(64, mx), imag.reshape(64, mx)], axis=0)
 
-    loads[4].wait()
+    loads[7].wait()
     both = dot3(tix_ref, modes, NT)
     cells = both[:half] - sign * pltpu.roll(both[half:], 64, 1)
-    send3[...] = cells.reshape(npx, XL, 128).astype(BF)
-    x_exchange(send3, recv3, ssem3, rsem3)
+    send3[...] = cells.reshape(xc, zc, XL, 128).astype(BF)
+    x_exchange(send3, mid3, recv3, sems3)
 
     block = recv3[...].astype(F32).reshape(half, 128)
     turned = jnp.concatenate([block, -sign * pltpu.roll(block, 64, 1)], axis=0)
@@ -297,7 +318,19 @@
         for core in range(2):
             y_arrive(send4, recv4, ssem4, rsem4, chip * 2 + core)
 
-    loads[5].wait()
+    def sent_y(d, carry):
+        target = lax.rem(mey + d, npy)
+        y_copy(send1, recv1, ssem1, rsem1, target).wait_send()
+        y_copy(send4, recv4, ssem4, rsem4, target).wait_send()
+        return carry
+
+    lax.fori_loop(1, npy, sent_y, 0)
+    for copy in sent:
+        copy.wait_send()
+
+
+def finish(npy, recv4, chan, b7_ref, out_hbm, done, sems):
+    copies = []
     for g in range(4):
         lines = jnp.concatenate(
             [recv4[:, 16 * g : 16 * g + 16, :].reshape(npy, 1, 16, 128),
@@ -306,22 +339,12 @@
         values = dot(lines, b7_ref[...], TN)
         for o in range(8):
             total = values[:, 128 * o : 128 * o + 128] + chan[8 * g + o]
-            out_ref[8 * g + o] = gelu(total).astype(BF)
-
-    def sent_y(d, carry):
-        target = lax.rem(mey + d, npy)
-        y_copy(send1, recv1, ssem1, rsem1, target).wait_send()
-        y_copy(send4, recv4, ssem4, rsem4, target).wait_send()
-        return carry
-
-    def sent_x(d, carry):
-        target = lax.rem(mex + d, npx)
-        x_copy(send2, recv2, ssem2, rsem2, target).wait_send()
-        x_copy(send3, recv3, ssem3, rsem3, target).wait_send()
-        return carry
-
-    lax.fori_loop(1, npy, sent_y, 0)
-    lax.fori_loop(1, npx, sent_x, 0)
+            done[8 * g + o] = gelu(total).astype(BF)
+        block = pl.ds(8 * g, 8)
+        copies.append(pltpu.make_async_copy(done.at[block], out_hbm.at[block], sems.at[g]))
+        copies[-1].start()
+    for copy in copies:
+        copy.wait()
 
 
 def body(npx, npy, field, spec_weight, w_in, b_in, w_out):
@@ -330,50 +353,54 @@
     cells = field.reshape(C, XL * YL, NZ)
     weight = jnp.transpose(spec_weight[0], (0, 1, 2, 4, 5, 3)).reshape(2, C, C * K2, mx)
     vmem = pl.BlockSpec(memory_space=pltpu.VMEM)
-    anywhere = pl.BlockSpec(memory_space=pl.ANY)
-    out = pl.pallas_call(
+    hbm = pl.BlockSpec(memory_space=pltpu.HBM)
+    xc, zc = chips(npx)
+    exchange = [pltpu.VMEM((xc, zc, XL, 128), BF)] * 3
+    loaded = [
+        cells, jnp.asarray(a1), w_in[0], b_in, jnp.transpose(w_out[0]), weight,
+        jnp.asarray(a2), jnp.asarray(tx), jnp.asarray(tix), jnp.asarray(e8),
+    ]
+    loaded = [pltpu.with_memory_space_constraint(a, pltpu.HBM) for a in loaded]
+    lines, chan = pl.pallas_call(
         functools.partial(kernel, npx, npy),
-        out_shape=jax.ShapeDtypeStruct((C, XL * YL, NZ), BF),
-        in_specs=[vmem] * 5 + [anywhere] * 6,
-        out_specs=vmem,
+        out_shape=(
+            pltpu.VMEM((npy, 128, 128), BF),
+            pltpu.VMEM((C, XL * YL, NZ), F32),
+        ),
+        in_specs=[hbm] * len(loaded),
+        out_specs=(vmem, vmem),
         scratch_shapes=[
             pltpu.VMEM((npy, 2, 8, 8, 128), F32),
             pltpu.VMEM((npy, 128, 128), BF),
             pltpu.VMEM((npy, 128, 128), BF),
-            pltpu.VMEM((npx, XL, 128), BF),
-            pltpu.VMEM((npx, XL, 128), BF),
-            pltpu.VMEM((npx, XL, 128), BF),
-            pltpu.VMEM((npx, XL, 128), BF),
+            *exchange,
+            *exchange,
             pltpu.VMEM((npy, 128, 128), BF),
-            pltpu.VMEM((npy, 128, 128), BF),
-            pltpu.VMEM(weight.shape, BF),
-            pltpu.VMEM(a2.shape, BF),
-            pltpu.VMEM(tx.shape, BF),
-            pltpu.VMEM(tix.shape, BF),
-            pltpu.VMEM(b7.shape, BF),
-            pltpu.VMEM(e8.shape, BF),
+            *[pltpu.VMEM(a.shape, a.dtype) for a in loaded],
             pltpu.VMEM((HID * 8, C * 8), BF),
             pltpu.VMEM((C * 8, HID * 8), BF),
             pltpu.VMEM((HID * 8, 128), F32),
-            pltpu.VMEM((C, XL * YL, NZ), F32),
             pltpu.VMEM((2 * C, 8, mx), F32),
             pltpu.SemaphoreType.DMA((npy,)),
             pltpu.SemaphoreType.DMA((npy,)),
-            pltpu.SemaphoreType.DMA((npx,)),
-            pltpu.SemaphoreType.DMA((npx,)),
-            pltpu.SemaphoreType.DMA((npx,)),
-            pltpu.SemaphoreType.DMA((npx,)),
+            pltpu.SemaphoreType.DMA((4, max(xc, zc))),
+            pltpu.SemaphoreType.DMA((4, max(xc, zc))),
             pltpu.SemaphoreType.DMA((npy,)),
             pltpu.SemaphoreType.DMA((npy,)),
-            pltpu.SemaphoreType.DMA((6,)),
+            pltpu.SemaphoreType.DMA((13,)),
         ],
         compiler_params=pltpu.CompilerParams(
-            collective_id=0, has_side_effects=True, vmem_limit_bytes=60 * 1024 * 1024
+            collective_id=0, has_side_effects=True, vmem_limit_bytes=32 * 1024 * 1024
         ),
-    )(
-        cells, jnp.asarray(a1), w_in[0], b_in, jnp.transpose(w_out[0]), weight,
-        jnp.asarray(a2), jnp.asarray(tx), jnp.asarray(tix), jnp.asarray(b7), jnp.asarray(e8),
-    )
+    )(*loaded)
+    out = pl.pallas_call(
+        functools.partial(finish, npy),
+        out_shape=jax.ShapeDtypeStruct((C, XL * YL, NZ), BF),
+        in_specs=[vmem] * 3,
+        out_specs=hbm,
+        scratch_shapes=[pltpu.VMEM((C, XL * YL, NZ), BF), pltpu.SemaphoreType.DMA((4,))],
+        compiler_params=pltpu.CompilerParams(vmem_limit_bytes=16 * 1024 * 1024),
+    )(lines, chan, jnp.asarray(b7))
     return out.reshape(field.shape)
 
 

time: 65.1 us -> 62 us (0.952)
  local copies, waits for them, and re-layouts: 2.49 us -> 0.01 us
    unnamed x1 -> x2, local copies, waits for them, and re-layouts: 2.49 us -> 0.01 us
    pallas_call x1 -> x2, Pallas kernels: 62.4 us -> 61.9 us  [the longest x1 60 us: body(): pl.pallas_call(functools.partial(kernel, npx, npy), out_shape=(pltpu.VMEM...]
where the time goes in v2:
time: 62 us; the launch traced here: 61.9 us
  Pallas kernels  61.9 us (100%)
    pallas_call x1, Pallas kernels, body(): pl.pallas_call(functools.partial(kernel, npx, npy), out_shape=(pltpu.VMEM...  60 us
    pallas_call x1, Pallas kernels, body(): pl.pallas_call(functools.partial(finish, npy), out_shape=jax.ShapeDtypeSt...  1.94 us

profile of v2, /device:TPU:1, one launch (start us, length us, event | category | flops | bytes accessed | tf_op | source)
XLA Modules:
  0.0 61.9 jit_solution(8937019872640471539)
XLA Ops:
  0.0 0.0 copy-start
  0.0 60.0 %shard_map.109 = (bf16[16,128,128]{2,1,0:T(8,128)(2,1)S(1)}, f32[32,128,128]{2,1,0:T(8,128)S(1)}) custom-call(bf16[32,128,128]{2,1,0:T(8,128)(2,1)} %bitcast.11, bf16[2,256,256]{2,1,0:T(8,128)(2,1)} %constant.12.clone.a1_hbm, bf16[32,128]{1,0:T(8,128)(2,1)} %bitcast.13, f32[1,128]{1,0:T(1,128)} %bin_hbm.1, bf16[32,128]{1,0:T(8,128)(2,1)} %bitcast.14, ...), custom_call_target="tpu_custom_call" | custom-call | tf_op jit(solution)/shard_map/pallas_call | solution.py:364
  60.0 0.0 copy-done
  60.0 1.9 %shard_map.110 = bf16[32,128,128]{2,1,0:T(8,128)(2,1)} custom-call(bf16[16,128,128]{2,1,0:T(8,128)(2,1)S(1)} %get-tuple-element.7.recv4, f32[32,128,128]{2,1,0:T(8,128)S(1)} %get-tuple-element.8.chan, bf16[512,1024]{1,0:T(8,128)(2,1)S(1)} %copy-done), custom_call_target="tpu_custom_call" | custom-call | tf_op jit(solution)/shard_map/pallas_call | solution.py:396
Async XLA Ops:
  0.0 60.0 %copy-start = (bf16[512,1024]{1,0:T(8,128)(2,1)S(1)}, bf16[512,1024]{1,0:T(8,128)(2,1)}, u32[]{:S(2)}) copy-start(bf16[512,1024]{1,0:T(8,128)(2,1)} %constant.17.clone.b7_ref) | copy-start | bytes 3145732

commit v3 on v2

--- a/solution.py
+++ b/solution.py
@@ -22,11 +22,6 @@
 NT = (((1,), (1,)), ((), ()))
 NN = (((1,), (0,)), ((), ()))
 TN = (((0,), (0,)), ((), ()))
-
-
-def chips(npx):
-    zc = max(npx // 4, min(npx, 2))
-    return npx // zc, zc
 
 
 def dot(a, b, dims):
@@ -105,22 +100,19 @@
     npx, npy,
     f_hbm, a1_hbm, win_hbm, bin_hbm, wout_hbm, w_hbm, a2_hbm, tx_hbm, tix_hbm, e8_hbm,
     recv4, chan,
-    zs, send1, recv1, send2, mid2, recv2, send3, mid3, recv3, send4,
+    zs, send1, recv1, send2, recv2, send3, recv3, send4,
     f_ref, a1_ref, win_ref, bin_ref, wout_ref, w_ref, a2_ref, tx_ref, tix_ref, e8_ref,
     k1, k2, bias, xpat,
     ssem1, rsem1, sems2, sems3, ssem4, rsem4, tsem,
 ):
     ny = npy // 2
     mx = w_ref.shape[-1]
-    xc, zc = chips(npx)
     sent = []
     mex = lax.axis_index("px")
     mey = lax.axis_index("py")
     my_chip = mey // 2
     my_core = mey % 2
     twin = my_chip * 2 + 1 - my_core
-    mex_x = mex // zc
-    mex_z = mex % zc
 
     def load(i, src, dst):
         return pltpu.make_async_copy(src, dst, tsem.at[i])
@@ -133,21 +125,14 @@
     loads = [load(5 + i, src, dst) for i, (src, dst) in enumerate(pairs)]
     barrier = pltpu.get_barrier_semaphore()
 
-    def greet_y(d, carry):
-        pl.semaphore_signal(barrier, inc=1, device_id=(mex, lax.rem(mey + d, npy)), device_id_type=MESH)
-        return carry
-
     for load in cells_in + loads:
         load.start()
-    lax.fori_loop(1, npy, greet_y, 0)
-    for d in range(1, zc):
-        pl.semaphore_signal(
-            barrier, inc=1, device_id=(mex_x * zc + lax.rem(mex_z + d, zc), mey), device_id_type=MESH
-        )
-    for d in range(1, xc):
-        pl.semaphore_signal(
-            barrier, inc=1, device_id=(lax.rem(mex_x + d, xc) * zc + mex_z, mey), device_id_type=MESH
-        )
+    x_peers = [(mex + d) & (npx - 1) for d in range(1, npx)]
+    y_peers_all = [(mey + d) & (npy - 1) for d in range(1, npy)]
+    for peer in y_peers_all:
+        pl.semaphore_signal(barrier, inc=1, device_id=(mex, peer), device_id_type=MESH)
+    for peer in x_peers:
+        pl.semaphore_signal(barrier, inc=1, device_id=(peer, mey), device_id_type=MESH)
 
     def forward_z(g, carry):
         f4 = f_ref[pl.ds(g * 4, 4)]
@@ -162,7 +147,7 @@
         lax.fori_loop(2 * i, 2 * i + 2, forward_z, 0, unroll=2)
     send1[...] = zs[...].reshape(npy, 128, 128).astype(BF)
 
-    pl.semaphore_wait(barrier, npy + zc + xc - 3)
+    pl.semaphore_wait(barrier, npy + npx - 2)
 
     def y_copy(src, dst, ssem, rsem, target):
         return pltpu.make_async_remote_copy(
@@ -176,30 +161,19 @@
             device_id=(mex, source), device_id_type=MESH,
         ).wait_recv()
 
-    def x_exchange(src, mid, dst, sems):
-        def hop(first, target, slot):
-            if first:
-                return pltpu.make_async_remote_copy(
-                    src_ref=src.at[:, target], dst_ref=mid.at[:, slot], send_sem=sems.at[0, target],
-                    recv_sem=sems.at[1, slot], device_id=(mex_x * zc + target, mey), device_id_type=MESH,
-                )
-            return pltpu.make_async_remote_copy(
-                src_ref=mid.at[target], dst_ref=dst.at[slot], send_sem=sems.at[2, target],
-                recv_sem=sems.at[3, slot], device_id=(target * zc + mex_z, mey), device_id_type=MESH,
-            )
-
-        for first, own, count in ((True, mex_z, zc), (False, mex_x, xc)):
-            others = [lax.rem(own + d, count) for d in sorted(range(1, count), key=lambda d: -min(d, count - d))]
-            for other in others:
-                hop(first, other, own).start()
-            if first:
-                mid[:, pl.ds(own, 1)] = src[:, pl.ds(own, 1)]
-            else:
-                dst[pl.ds(own, 1)] = mid[pl.ds(own, 1)]
-            for other in others:
-                hop(first, other, other).wait_recv()
-            for other in others:
-                sent.append(hop(first, other, own))
+    def x_exchange(src, dst, sems):
+        for other in x_peers:
+            pltpu.make_async_remote_copy(
+                src_ref=src.at[other], dst_ref=dst.at[mex], send_sem=sems.at[0], recv_sem=sems.at[1],
+                device_id=(other, mey), device_id_type=MESH,
+            ).start()
+        dst[pl.ds(mex, 1)] = src[pl.ds(mex, 1)]
+        whole = pltpu.make_async_remote_copy(
+            src_ref=src.at[pl.ds(0, npx - 1)], dst_ref=dst.at[pl.ds(0, npx - 1)], send_sem=sems.at[0],
+            recv_sem=sems.at[1], device_id=(x_peers[0], mey), device_id_type=MESH,
+        )
+        whole.wait_recv()
+        sent.append(whole)
 
     def y_peers(far_first):
         offsets = sorted(range(1, ny), key=lambda d: min(d, ny - d), reverse=far_first)
@@ -263,8 +237,8 @@
         acc = acc + y_part(chip)
     half = npx * XL
     lines = acc[:half] + sign * pltpu.roll(acc[half:], 64, 1)
-    send2[...] = lines.reshape(xc, zc, XL, 128).astype(BF)
-    x_exchange(send2, mid2, recv2, sems2)
+    send2[...] = lines.reshape(npx, XL, 128).astype(BF)
+    x_exchange(send2, recv2, sems2)
 
     loads[4].wait()
     loads[5].wait()
@@ -291,8 +265,8 @@
     loads[7].wait()
     both = dot3(tix_ref, modes, NT)
     cells = both[:half] - sign * pltpu.roll(both[half:], 64, 1)
-    send3[...] = cells.reshape(xc, zc, XL, 128).astype(BF)
-    x_exchange(send3, mid3, recv3, sems3)
+    send3[...] = cells.reshape(npx, XL, 128).astype(BF)
+    x_exchange(send3, recv3, sems3)
 
     block = recv3[...].astype(F32).reshape(half, 128)
     turned = jnp.concatenate([block, -sign * pltpu.roll(block, 64, 1)], axis=0)
@@ -354,8 +328,7 @@
     weight = jnp.transpose(spec_weight[0], (0, 1, 2, 4, 5, 3)).reshape(2, C, C * K2, mx)
     vmem = pl.BlockSpec(memory_space=pltpu.VMEM)
     hbm = pl.BlockSpec(memory_space=pltpu.HBM)
-    xc, zc = chips(npx)
-    exchange = [pltpu.VMEM((xc, zc, XL, 128), BF)] * 3
+    exchange = [pltpu.VMEM((npx, XL, 128), BF)] * 2
     loaded = [
         cells, jnp.asarray(a1), w_in[0], b_in, jnp.transpose(w_out[0]), weight,
         jnp.asarray(a2), jnp.asarray(tx), jnp.asarray(tix), jnp.asarray(e8),
@@ -383,8 +356,8 @@
             pltpu.VMEM((2 * C, 8, mx), F32),
             pltpu.SemaphoreType.DMA((npy,)),
             pltpu.SemaphoreType.DMA((npy,)),
-            pltpu.SemaphoreType.DMA((4, max(xc, zc))),
-            pltpu.SemaphoreType.DMA((4, max(xc, zc))),
+            pltpu.SemaphoreType.DMA((2,)),
+            pltpu.SemaphoreType.DMA((2,)),
             pltpu.SemaphoreType.DMA((npy,)),
             pltpu.SemaphoreType.DMA((npy,)),
             pltpu.SemaphoreType.DMA((13,)),

time: 62 us -> 59.5 us (0.960)
  Pallas kernels: 61.9 us -> 59.4 us
    pallas_call x1, Pallas kernels: 60 us -> 57.5 us  [body(): pl.pallas_call(functools.partial(kernel, npx, npy), out_shape=(pltpu.VMEM...]
where the time goes in v3:
time: 59.5 us; the launch traced here: 59.4 us
  Pallas kernels  59.4 us (100%)
    pallas_call x1, Pallas kernels, body(): pl.pallas_call(functools.partial(kernel, npx, npy), out_shape=(pltpu.VMEM...  57.5 us
    pallas_call x1, Pallas kernels, body(): pl.pallas_call(functools.partial(finish, npy), out_shape=jax.ShapeDtypeSt...  1.92 us

profile of v3, /device:TPU:1, one launch (start us, length us, event | category | flops | bytes accessed | tf_op | source)
XLA Modules:
  0.0 59.4 jit_solution(16887353129328115074)
XLA Ops:
  0.0 0.0 copy-start
  0.0 57.5 %shard_map.109 = (bf16[16,128,128]{2,1,0:T(8,128)(2,1)S(1)}, f32[32,128,128]{2,1,0:T(8,128)S(1)}) custom-call(bf16[32,128,128]{2,1,0:T(8,128)(2,1)} %bitcast.11, bf16[2,256,256]{2,1,0:T(8,128)(2,1)} %constant.12.clone.a1_hbm, bf16[32,128]{1,0:T(8,128)(2,1)} %bitcast.13, f32[1,128]{1,0:T(1,128)} %bin_hbm.1, bf16[32,128]{1,0:T(8,128)(2,1)} %bitcast.14, ...), custom_call_target="tpu_custom_call" | custom-call | tf_op jit(solution)/shard_map/pallas_call | solution.py:337
  57.5 0.0 copy-done
  57.5 1.9 %shard_map.110 = bf16[32,128,128]{2,1,0:T(8,128)(2,1)} custom-call(bf16[16,128,128]{2,1,0:T(8,128)(2,1)S(1)} %get-tuple-element.7.recv4, f32[32,128,128]{2,1,0:T(8,128)S(1)} %get-tuple-element.8.chan, bf16[512,1024]{1,0:T(8,128)(2,1)S(1)} %copy-done), custom_call_target="tpu_custom_call" | custom-call | tf_op jit(solution)/shard_map/pallas_call | solution.py:369
Async XLA Ops:
  0.0 57.5 %copy-start = (bf16[512,1024]{1,0:T(8,128)(2,1)S(1)}, bf16[512,1024]{1,0:T(8,128)(2,1)}, u32[]{:S(2)}) copy-start(bf16[512,1024]{1,0:T(8,128)(2,1)} %constant.17.clone.b7_ref) | copy-start | bytes 3145732

commit v4 on v3

--- a/solution.py
+++ b/solution.py
@@ -100,10 +100,10 @@
     npx, npy,
     f_hbm, a1_hbm, win_hbm, bin_hbm, wout_hbm, w_hbm, a2_hbm, tx_hbm, tix_hbm, e8_hbm,
     recv4, chan,
-    zs, send1, recv1, send2, recv2, send3, recv3, send4,
+    zs, send1, recv1, relay1, relay4, send2, recv2, send3, recv3, send4,
     f_ref, a1_ref, win_ref, bin_ref, wout_ref, w_ref, a2_ref, tx_ref, tix_ref, e8_ref,
     k1, k2, bias, xpat,
-    ssem1, rsem1, sems2, sems3, ssem4, rsem4, tsem,
+    ssem1, rsem1, rlsem1, sems2, sems3, ssem4, rsem4, rlsem4, tsem,
 ):
     ny = npy // 2
     mx = w_ref.shape[-1]
@@ -125,7 +125,7 @@
     loads = [load(5 + i, src, dst) for i, (src, dst) in enumerate(pairs)]
     barrier = pltpu.get_barrier_semaphore()
 
-    for load in cells_in + loads:
+    for load in cells_in:
         load.start()
     x_peers = [(mex + d) & (npx - 1) for d in range(1, npx)]
     y_peers_all = [(mey + d) & (npy - 1) for d in range(1, npy)]
@@ -145,6 +145,8 @@
     for i in range(4):
         cells_in[1 + i].wait()
         lax.fori_loop(2 * i, 2 * i + 2, forward_z, 0, unroll=2)
+    for load in loads:
+        load.start()
     send1[...] = zs[...].reshape(npy, 128, 128).astype(BF)
 
     pl.semaphore_wait(barrier, npy + npx - 2)
@@ -175,11 +177,38 @@
         whole.wait_recv()
         sent.append(whole)
 
+    step = ny // 4
+    quarter = [lax.rem(my_chip + step, ny) * 2 + my_core, lax.rem(my_chip + ny - step, ny) * 2 + my_core]
+    opposite = lax.rem(my_chip + ny // 2, ny) * 2
+
+    def to_relay(src, relay, sems, way):
+        return pltpu.make_async_remote_copy(
+            src_ref=src.at[opposite + way], dst_ref=relay.at[way], send_sem=sems.at[0, way], recv_sem=sems.at[1, way],
+            device_id=(mex, quarter[way]), device_id_type=MESH,
+        )
+
+    def from_relay(relay, dst, sems, rsem, way):
+        source = quarter[1 - way]
+        target = (quarter[way] - my_core) + way
+        return pltpu.make_async_remote_copy(
+            src_ref=relay.at[way], dst_ref=dst.at[source], send_sem=sems.at[2, way], recv_sem=rsem.at[source],
+            device_id=(mex, target), device_id_type=MESH,
+        )
+
+    def forward(src, relay, dst, sems, rsem):
+        for way in range(2):
+            to_relay(src, relay, sems, way).wait_recv()
+            from_relay(relay, dst, sems, rsem, way).start()
+            sent.append(to_relay(src, relay, sems, way))
+            sent.append(from_relay(relay, dst, sems, rsem, way))
+
     def y_peers(far_first):
         offsets = sorted(range(1, ny), key=lambda d: min(d, ny - d), reverse=far_first)
         return [lax.rem(my_chip + d, ny) for d in offsets]
 
-    for chip in y_peers(True):
+    for way in range(2):
+        to_relay(send1, relay1, rlsem1, way).start()
+    for chip in y_peers(True)[1:]:
         for core in range(2):
             y_copy(send1, recv1, ssem1, rsem1, chip * 2 + core).start()
     y_copy(send1, recv1, ssem1, rsem1, twin).start()
@@ -204,6 +233,8 @@
     turned = jnp.transpose(jnp.broadcast_to(bin_ref[...], (HID, HID)))
     bias[...] = jnp.broadcast_to(turned[:, None, :], (HID, 8, 128)).reshape(HID * 8, 128)
 
+    forward(send1, relay1, recv1, rlsem1, rsem1)
+
     def channel(i, carry):
         block = f_ref[:, pl.ds(pl.multiple_of(i * 16, 16), 16), :].astype(F32)
         cells = jnp.concatenate(
@@ -277,28 +308,33 @@
         send4[pl.ds(chip * 2, 1)] = both[:, :128][None]
         send4[pl.ds(chip * 2 + 1, 1)] = both[:, 128:][None]
 
-    for chip in y_peers(True):
+    for i, chip in enumerate(y_peers(True)):
         y_back(chip)
         for core in range(2):
-            y_copy(send4, recv4, ssem4, rsem4, chip * 2 + core).start()
+            if i:
+                y_copy(send4, recv4, ssem4, rsem4, chip * 2 + core).start()
+            else:
+                to_relay(send4, relay4, rlsem4, core).start()
     y_back(my_chip)
     y_copy(send4, recv4, ssem4, rsem4, twin).start()
     recv4[pl.ds(mey, 1)] = send4[pl.ds(mey, 1)]
 
-    lax.fori_loop(4, 8, channel, 0)
+    channel(4, 0)
+    channel(5, 0)
+    forward(send4, relay4, recv4, rlsem4, rsem4)
+    lax.fori_loop(6, 8, channel, 0)
 
     y_arrive(send4, recv4, ssem4, rsem4, twin)
     for chip in y_peers(False):
         for core in range(2):
             y_arrive(send4, recv4, ssem4, rsem4, chip * 2 + core)
 
-    def sent_y(d, carry):
-        target = lax.rem(mey + d, npy)
-        y_copy(send1, recv1, ssem1, rsem1, target).wait_send()
-        y_copy(send4, recv4, ssem4, rsem4, target).wait_send()
-        return carry
-
-    lax.fori_loop(1, npy, sent_y, 0)
+    sent.append(y_copy(send1, recv1, ssem1, rsem1, twin))
+    sent.append(y_copy(send4, recv4, ssem4, rsem4, twin))
+    for chip in y_peers(True)[1:]:
+        for core in range(2):
+            sent.append(y_copy(send1, recv1, ssem1, rsem1, chip * 2 + core))
+            sent.append(y_copy(send4, recv4, ssem4, rsem4, chip * 2 + core))
     for copy in sent:
         copy.wait_send()
 
@@ -346,6 +382,8 @@
             pltpu.VMEM((npy, 2, 8, 8, 128), F32),
             pltpu.VMEM((npy, 128, 128), BF),
             pltpu.VMEM((npy, 128, 128), BF),
+            pltpu.VMEM((2, 128, 128), BF),
+            pltpu.VMEM((2, 128, 128), BF),
             *exchange,
             *exchange,
             pltpu.VMEM((npy, 128, 128), BF),
@@ -356,10 +394,12 @@
             pltpu.VMEM((2 * C, 8, mx), F32),
             pltpu.SemaphoreType.DMA((npy,)),
             pltpu.SemaphoreType.DMA((npy,)),
+            pltpu.SemaphoreType.DMA((3, 2)),
             pltpu.SemaphoreType.DMA((2,)),
             pltpu.SemaphoreType.DMA((2,)),
             pltpu.SemaphoreType.DMA((npy,)),
             pltpu.SemaphoreType.DMA((npy,)),
+            pltpu.SemaphoreType.DMA((3, 2)),
             pltpu.SemaphoreType.DMA((13,)),
         ],
         compiler_params=pltpu.CompilerParams(

time: 59.5 us -> 58.5 us (0.983)
  Pallas kernels: 59.4 us -> 58.3 us
    pallas_call x1, Pallas kernels: 57.5 us -> 56.4 us  [body(): pl.pallas_call(functools.partial(kernel, npx, npy), out_shape=(pltpu.VMEM...]
where the time goes in v4:
time: 58.5 us; the launch traced here: 58.3 us
  Pallas kernels  58.3 us (100%)
    pallas_call x1, Pallas kernels, body(): pl.pallas_call(functools.partial(kernel, npx, npy), out_shape=(pltpu.VMEM...  56.4 us
    pallas_call x1, Pallas kernels, body(): pl.pallas_call(functools.partial(finish, npy), out_shape=jax.ShapeDtypeSt...  1.93 us

profile of v4, /device:TPU:1, one launch (start us, length us, event | category | flops | bytes accessed | tf_op | source)
XLA Modules:
  0.0 58.3 jit_solution(8924253783797503910)
XLA Ops:
  0.0 0.0 copy-start
  0.0 56.4 %shard_map.109 = (bf16[16,128,128]{2,1,0:T(8,128)(2,1)S(1)}, f32[32,128,128]{2,1,0:T(8,128)S(1)}) custom-call(bf16[32,128,128]{2,1,0:T(8,128)(2,1)} %bitcast.11, bf16[2,256,256]{2,1,0:T(8,128)(2,1)} %constant.12.clone.a1_hbm, bf16[32,128]{1,0:T(8,128)(2,1)} %bitcast.13, f32[1,128]{1,0:T(1,128)} %bin_hbm.1, bf16[32,128]{1,0:T(8,128)(2,1)} %bitcast.14, ...), custom_call_target="tpu_custom_call" | custom-call | tf_op jit(solution)/shard_map/pallas_call | solution.py:373
  56.4 0.0 copy-done
  56.4 1.9 %shard_map.110 = bf16[32,128,128]{2,1,0:T(8,128)(2,1)} custom-call(bf16[16,128,128]{2,1,0:T(8,128)(2,1)S(1)} %get-tuple-element.7.recv4, f32[32,128,128]{2,1,0:T(8,128)S(1)} %get-tuple-element.8.chan, bf16[512,1024]{1,0:T(8,128)(2,1)S(1)} %copy-done), custom_call_target="tpu_custom_call" | custom-call | tf_op jit(solution)/shard_map/pallas_call | solution.py:409
Async XLA Ops:
  0.0 56.4 %copy-start = (bf16[512,1024]{1,0:T(8,128)(2,1)S(1)}, bf16[512,1024]{1,0:T(8,128)(2,1)}, u32[]{:S(2)}) copy-start(bf16[512,1024]{1,0:T(8,128)(2,1)} %constant.17.clone.b7_ref) | copy-start | bytes 3145732

commit v5 on v4

--- a/solution.py
+++ b/solution.py
@@ -73,21 +73,7 @@
     def half(t):
         return t.astype(np.float32).astype(ml_dtypes.bfloat16)
 
-    def two(t):
-        high = half(t)
-        return np.stack([high, half(t - high.astype(np.float64))])
-
-    return half(a1), half(a2), two(tx), two(tix), half(b7), half(e8)
-
-
-def split(value):
-    high = value.astype(BF)
-    return high, (value - high.astype(F32)).astype(BF)
-
-
-def dot3(table, value, dims):
-    high, low = split(value)
-    return dot(table[0], high, dims) + dot(table[0], low, dims) + dot(table[1], high, dims)
+    return half(a1), half(a2), half(tx), half(tix), half(b7), half(e8)
 
 
 def gelu(v):
@@ -151,15 +137,21 @@
 
     pl.semaphore_wait(barrier, npy + npx - 2)
 
-    def y_copy(src, dst, ssem, rsem, target):
+    def y_copy(src, dst, ssem, rsem, target, many=True):
         return pltpu.make_async_remote_copy(
-            src_ref=src.at[target], dst_ref=dst.at[mey], send_sem=ssem.at[target], recv_sem=rsem.at[mey],
-            device_id=(mex, target), device_id_type=MESH,
+            src_ref=src.at[target], dst_ref=dst.at[mey], send_sem=ssem.at[0],
+            recv_sem=rsem.at[mey if many else 0], device_id=(mex, target), device_id_type=MESH,
+        )
+
+    def y_whole(src, dst, ssem, rsem):
+        return pltpu.make_async_remote_copy(
+            src_ref=src.at[pl.ds(0, npy - 1)], dst_ref=dst.at[pl.ds(0, npy - 1)], send_sem=ssem.at[0],
+            recv_sem=rsem.at[0], device_id=(mex, twin), device_id_type=MESH,
         )
 
     def y_arrive(src, dst, ssem, rsem, source):
         pltpu.make_async_remote_copy(
-            src_ref=src.at[source], dst_ref=dst.at[source], send_sem=ssem.at[source], recv_sem=rsem.at[source],
+            src_ref=src.at[source], dst_ref=dst.at[source], send_sem=ssem.at[0], recv_sem=rsem.at[source],
             device_id=(mex, source), device_id_type=MESH,
         ).wait_recv()
 
@@ -181,33 +173,33 @@
     quarter = [lax.rem(my_chip + step, ny) * 2 + my_core, lax.rem(my_chip + ny - step, ny) * 2 + my_core]
     opposite = lax.rem(my_chip + ny // 2, ny) * 2
 
-    def to_relay(src, relay, sems, way):
+    def to_relay(src, relay, ssem, sems, way):
         return pltpu.make_async_remote_copy(
-            src_ref=src.at[opposite + way], dst_ref=relay.at[way], send_sem=sems.at[0, way], recv_sem=sems.at[1, way],
+            src_ref=src.at[opposite + way], dst_ref=relay.at[way], send_sem=ssem.at[0], recv_sem=sems.at[1, way],
             device_id=(mex, quarter[way]), device_id_type=MESH,
         )
 
-    def from_relay(relay, dst, sems, rsem, way):
+    def from_relay(relay, dst, sems, rsem, way, many):
         source = quarter[1 - way]
         target = (quarter[way] - my_core) + way
         return pltpu.make_async_remote_copy(
-            src_ref=relay.at[way], dst_ref=dst.at[source], send_sem=sems.at[2, way], recv_sem=rsem.at[source],
+            src_ref=relay.at[way], dst_ref=dst.at[source], send_sem=sems.at[0, way],
+            recv_sem=rsem.at[source if many else 0],
             device_id=(mex, target), device_id_type=MESH,
         )
 
-    def forward(src, relay, dst, sems, rsem):
+    def forward(src, relay, dst, ssem, sems, rsem, many):
         for way in range(2):
-            to_relay(src, relay, sems, way).wait_recv()
-            from_relay(relay, dst, sems, rsem, way).start()
-            sent.append(to_relay(src, relay, sems, way))
-            sent.append(from_relay(relay, dst, sems, rsem, way))
+            to_relay(src, relay, ssem, sems, way).wait_recv()
+            from_relay(relay, dst, sems, rsem, way, many).start()
+            sent.append(from_relay(relay, dst, sems, rsem, way, many))
 
     def y_peers(far_first):
         offsets = sorted(range(1, ny), key=lambda d: min(d, ny - d), reverse=far_first)
         return [lax.rem(my_chip + d, ny) for d in offsets]
 
     for way in range(2):
-        to_relay(send1, relay1, rlsem1, way).start()
+        to_relay(send1, relay1, ssem1, rlsem1, way).start()
     for chip in y_peers(True)[1:]:
         for core in range(2):
             y_copy(send1, recv1, ssem1, rsem1, chip * 2 + core).start()
@@ -233,7 +225,7 @@
     turned = jnp.transpose(jnp.broadcast_to(bin_ref[...], (HID, HID)))
     bias[...] = jnp.broadcast_to(turned[:, None, :], (HID, 8, 128)).reshape(HID * 8, 128)
 
-    forward(send1, relay1, recv1, rlsem1, rsem1)
+    forward(send1, relay1, recv1, ssem1, rlsem1, rsem1, True)
 
     def channel(i, carry):
         block = f_ref[:, pl.ds(pl.multiple_of(i * 16, 16), 16), :].astype(F32)
@@ -274,10 +266,9 @@
     loads[4].wait()
     loads[5].wait()
     block = recv2[...].astype(F32).reshape(half, 128).astype(BF)
-    both = dot(tx_ref[0], block, NN) + dot(tx_ref[1], block, NN)
+    both = dot(tx_ref[...], block, NN)
     spectra = both[:mx] + sign * pltpu.roll(both[mx:], 64, 1)
-    high, low = split(spectra)
-    xpat[...] = (dot(e8_ref[...], high, NT) + dot(e8_ref[...], low, NT)).reshape(2 * C, 8, mx)
+    xpat[...] = dot(e8_ref[...], spectra.astype(BF), NT).reshape(2 * C, 8, mx)
 
     loads[6].wait()
 
@@ -294,14 +285,15 @@
     modes = jnp.concatenate([real.reshape(64, mx), imag.reshape(64, mx)], axis=0)
 
     loads[7].wait()
-    both = dot3(tix_ref, modes, NT)
+    both = dot(tix_ref[...], modes.astype(BF), NT)
     cells = both[:half] - sign * pltpu.roll(both[half:], 64, 1)
     send3[...] = cells.reshape(npx, XL, 128).astype(BF)
     x_exchange(send3, recv3, sems3)
 
-    block = recv3[...].astype(F32).reshape(half, 128)
-    turned = jnp.concatenate([block, -sign * pltpu.roll(block, 64, 1)], axis=0)
-    turned = jnp.transpose(turned).astype(BF)
+    turned = jnp.transpose(recv3[...].astype(F32).reshape(half, 128))
+    turned = jnp.concatenate(
+        [turned, jnp.concatenate([-turned[64:], turned[:64]], axis=0)], axis=1
+    ).astype(BF)
 
     def y_back(chip):
         both = dot(turned, a2_ref[chip], NN).astype(BF)
@@ -312,29 +304,24 @@
         y_back(chip)
         for core in range(2):
             if i:
-                y_copy(send4, recv4, ssem4, rsem4, chip * 2 + core).start()
+                y_copy(send4, recv4, ssem4, rsem4, chip * 2 + core, False).start()
             else:
-                to_relay(send4, relay4, rlsem4, core).start()
+                to_relay(send4, relay4, ssem4, rlsem4, core).start()
     y_back(my_chip)
-    y_copy(send4, recv4, ssem4, rsem4, twin).start()
+    y_copy(send4, recv4, ssem4, rsem4, twin, False).start()
     recv4[pl.ds(mey, 1)] = send4[pl.ds(mey, 1)]
 
     channel(4, 0)
     channel(5, 0)
-    forward(send4, relay4, recv4, rlsem4, rsem4)
+    sent.append(y_whole(send1, recv1, ssem1, rsem1))
+    for copy in sent:
+        copy.wait_send()
+    sent.clear()
+    forward(send4, relay4, recv4, ssem4, rlsem4, rsem4, False)
     lax.fori_loop(6, 8, channel, 0)
 
-    y_arrive(send4, recv4, ssem4, rsem4, twin)
-    for chip in y_peers(False):
-        for core in range(2):
-            y_arrive(send4, recv4, ssem4, rsem4, chip * 2 + core)
-
-    sent.append(y_copy(send1, recv1, ssem1, rsem1, twin))
-    sent.append(y_copy(send4, recv4, ssem4, rsem4, twin))
-    for chip in y_peers(True)[1:]:
-        for core in range(2):
-            sent.append(y_copy(send1, recv1, ssem1, rsem1, chip * 2 + core))
-            sent.append(y_copy(send4, recv4, ssem4, rsem4, chip * 2 + core))
+    y_whole(send4, recv4, ssem4, rsem4).wait_recv()
+    sent.append(y_whole(send4, recv4, ssem4, rsem4))
     for copy in sent:
         copy.wait_send()
 
@@ -392,14 +379,14 @@
             pltpu.VMEM((C * 8, HID * 8), BF),
             pltpu.VMEM((HID * 8, 128), F32),
             pltpu.VMEM((2 * C, 8, mx), F32),
+            pltpu.SemaphoreType.DMA((1,)),
             pltpu.SemaphoreType.DMA((npy,)),
-            pltpu.SemaphoreType.DMA((npy,)),
-            pltpu.SemaphoreType.DMA((3, 2)),
+            pltpu.SemaphoreType.DMA((2, 2)),
             pltpu.SemaphoreType.DMA((2,)),
             pltpu.SemaphoreType.DMA((2,)),
-            pltpu.SemaphoreType.DMA((npy,)),
-            pltpu.SemaphoreType.DMA((npy,)),
-            pltpu.SemaphoreType.DMA((3, 2)),
+            pltpu.SemaphoreType.DMA((1,)),
+            pltpu.SemaphoreType.DMA((1,)),
+            pltpu.SemaphoreType.DMA((2, 2)),
             pltpu.SemaphoreType.DMA((13,)),
         ],
         compiler_params=pltpu.CompilerParams(

time: 58.5 us -> 57.8 us (0.988)
  Pallas kernels: 58.3 us -> 57.6 us
    pallas_call x1, Pallas kernels: 56.4 us -> 55.6 us  [body(): pl.pallas_call(functools.partial(kernel, npx, npy), out_shape=(pltpu.VMEM...]
where the time goes in v5:
time: 57.8 us; the launch traced here: 57.6 us
  Pallas kernels  57.6 us (100%)
    pallas_call x1, Pallas kernels, body(): pl.pallas_call(functools.partial(kernel, npx, npy), out_shape=(pltpu.VMEM...  55.6 us
    pallas_call x1, Pallas kernels, body(): pl.pallas_call(functools.partial(finish, npy), out_shape=jax.ShapeDtypeSt...  1.93 us

profile of v5, /device:TPU:1, one launch (start us, length us, event | category | flops | bytes accessed | tf_op | source)
XLA Modules:
  0.0 57.6 jit_solution(10394090694199253063)
XLA Ops:
  0.0 0.0 copy-start
  0.0 55.6 %shard_map.109 = (bf16[16,128,128]{2,1,0:T(8,128)(2,1)S(1)}, f32[32,128,128]{2,1,0:T(8,128)S(1)}) custom-call(bf16[32,128,128]{2,1,0:T(8,128)(2,1)} %bitcast.11, bf16[2,256,256]{2,1,0:T(8,128)(2,1)} %constant.12.clone.a1_hbm, bf16[32,128]{1,0:T(8,128)(2,1)} %bitcast.13, f32[1,128]{1,0:T(1,128)} %bin_hbm.1, bf16[32,128]{1,0:T(8,128)(2,1)} %bitcast.14, ...), custom_call_target="tpu_custom_call" | custom-call | tf_op jit(solution)/shard_map/pallas_call | solution.py:360
  55.6 0.0 copy-done
  55.7 1.9 %shard_map.110 = bf16[32,128,128]{2,1,0:T(8,128)(2,1)} custom-call(bf16[16,128,128]{2,1,0:T(8,128)(2,1)S(1)} %get-tuple-element.7.recv4, f32[32,128,128]{2,1,0:T(8,128)S(1)} %get-tuple-element.8.chan, bf16[512,1024]{1,0:T(8,128)(2,1)S(1)} %copy-done), custom_call_target="tpu_custom_call" | custom-call | tf_op jit(solution)/shard_map/pallas_call | solution.py:396
Async XLA Ops:
  0.0 55.6 %copy-start = (bf16[512,1024]{1,0:T(8,128)(2,1)S(1)}, bf16[512,1024]{1,0:T(8,128)(2,1)}, u32[]{:S(2)}) copy-start(bf16[512,1024]{1,0:T(8,128)(2,1)} %constant.17.clone.b7_ref) | copy-start | bytes 3145732

commit v6 on v3

v6 whole, which is shorter than its diff:
```python
import functools
import math

import jax
import jax.numpy as jnp
import ml_dtypes
import numpy as np
from jax import lax
from jax.experimental import pallas as pl
from jax.experimental.pallas import tpu as pltpu
from jax.sharding import PartitionSpec as P

MESH = pl.DeviceIdType.MESH
BF = jnp.bfloat16
F32 = jnp.float32
C = 32
HID = 128
XL = 8
YL = 16
NZ = 128
K2 = 2
NT = (((1,), (1,)), ((), ()))
NN = (((1,), (0,)), ((), ()))
TN = (((0,), (0,)), ((), ()))


def dot(a, b, dims):
    return lax.dot_general(a, b, dims, preferred_element_type=F32)


def signed(count, length):
    index = np.arange(count)
    return np.where(index < count // 2, index, index - count + length)


def angles(positions, freqs, length):
    return 2.0 * math.pi * ((positions[:, None] * freqs[None, :]) % length) / length


def tables(npx, npy, mx):
    nx, ny, my, mz = XL * npx, YL * npy, npx, K2 * npy
    ang = angles(np.arange(NZ), np.arange(mz), NZ)
    fwd = np.stack([np.cos(ang), -np.sin(ang)]) * 0.125
    fwd = fwd.reshape(2, NZ, npy, K2).transpose(2, 3, 0, 1)
    a1 = np.zeros((2, npy, K2, 2, 4, 2, NZ))
    for q in range(2):
        for c in range(2):
            a1[q, :, :, :, 2 * q + c, c, :] = fwd
    a1 = a1.reshape(2, npy * 16, 2 * NZ)
    ang = angles(np.arange(ny), signed(my, ny), ny)
    cs = np.stack([np.cos(ang), np.sin(ang)]).reshape(2, npy // 2, 2, YL, my)
    a2 = np.zeros((npy // 2, 2, my, XL, 2, XL, YL))
    for x in range(XL):
        a2[:, :, :, x, :, x, :] = cs.transpose(1, 0, 4, 2, 3)
    a2 = a2.reshape(npy // 2, 2 * my * XL, 2 * XL * YL)
    ang = angles(np.arange(nx), signed(mx, nx), nx)
    cs = np.stack([np.cos(ang), np.sin(ang)])
    tx = cs.transpose(0, 2, 1).reshape(2 * mx, nx) / math.sqrt(nx * ny)
    tix = cs.reshape(2 * nx, mx) / math.sqrt(mx * my)
    ang = angles(np.arange(NZ), np.arange(mz), NZ)
    weight = np.where(np.arange(mz) == 0, 1.0, 2.0) * (8.0 / math.sqrt(NZ * mz))
    inv = np.stack([np.cos(ang), -np.sin(ang)]) * weight
    inv = inv.reshape(2, NZ, npy, K2).transpose(3, 2, 0, 1)
    b7 = np.zeros((K2, npy, 2, 2, 4, 8, NZ))
    for o in range(8):
        b7[:, :, o // 4, :, o % 4, o, :] = inv
    b7 = b7.reshape(npy * 32, 8 * NZ)
    e8 = np.zeros((2, C, 8, 2, C // 4, 2, 4))
    for c in range(C):
        for ri in range(2):
            e8[ri, c, :, 0, c // 4, ri, c % 4] = 1.0
    e8 = e8.reshape(2 * C * 8, 128)
    pick = np.zeros((K2, 2, C // 4, 2, 4, 2, C, K2))
    for o in range(C):
        for ri in range(2):
            for k in range(K2):
                pick[k, :, o // 4, ri, o % 4, ri, o, k] = 1.0
    pick = pick.reshape(K2, 128, 128)

    def half(t):
        return t.astype(np.float32).astype(ml_dtypes.bfloat16)

    return half(a1), half(a2), half(tx), half(tix), half(b7), half(e8), half(pick)


def gelu(v):
    k = math.sqrt(2.0 / math.pi)
    half = 0.5 * v
    return half + half * jnp.tanh(v * (k + (k * 0.044715) * (v * v)))


def kernel(
    npx, npy,
    f_hbm, a1_hbm, win_hbm, bin_hbm, wout_hbm, w_hbm, a2_hbm, tx_hbm, tix_hbm, e8_hbm, pick_hbm,
    recv4, chan,
    zs, send1, recv1, send2, recv2, send3, recv3, send4,
    f_ref, a1_ref, win_ref, bin_ref, wout_ref, w_ref, a2_ref, tx_ref, tix_ref, e8_ref, pick_ref,
    k1, k2, bias, xpat,
    ssem1, rsem1, sems2, sems3, ssem4, rsem4, tsem,
):
    ny = npy // 2
    mx = w_ref.shape[-1]
    sent = []
    mex = lax.axis_index("px")
    mey = lax.axis_index("py")
    my_chip = mey // 2
    my_core = mey % 2
    twin = my_chip * 2 + 1 - my_core

    def load(i, src, dst):
        return pltpu.make_async_copy(src, dst, tsem.at[i])

    cells_in = [load(0, a1_hbm, a1_ref)] + [
        load(1 + i, f_hbm.at[pl.ds(i * 8, 8)], f_ref.at[pl.ds(i * 8, 8)]) for i in range(4)
    ]
    pairs = [(win_hbm, win_ref), (bin_hbm, bin_ref), (wout_hbm, wout_ref), (a2_hbm, a2_ref), (tx_hbm, tx_ref),
             (e8_hbm, e8_ref), (w_hbm, w_ref), (tix_hbm, tix_ref), (pick_hbm, pick_ref)]
    loads = [load(5 + i, src, dst) for i, (src, dst) in enumerate(pairs)]
    barrier = pltpu.get_barrier_semaphore()

    for load in cells_in:
        load.start()
    x_peers = [(mex + d) & (npx - 1) for d in range(1, npx)]
    y_peers_all = [(mey + d) & (npy - 1) for d in range(1, npy)]
    for peer in y_peers_all:
        pl.semaphore_signal(barrier, inc=1, device_id=(mex, peer), device_id_type=MESH)
    for peer in x_peers:
        pl.semaphore_signal(barrier, inc=1, device_id=(peer, mey), device_id_type=MESH)

    def forward_z(g, carry):
        f4 = f_ref[pl.ds(g * 4, 4)]
        acc = dot(a1_ref[0], jnp.concatenate([f4[0], f4[1]], axis=1), NT)
        acc = acc + dot(a1_ref[1], jnp.concatenate([f4[2], f4[3]], axis=1), NT)
        zs[:, :, pl.ds(g, 1)] = acc.reshape(npy, K2, 1, 8, 128)
        return carry

    cells_in[0].wait()
    for i in range(4):
        cells_in[1 + i].wait()
        lax.fori_loop(2 * i, 2 * i + 2, forward_z, 0, unroll=2)
    for load in loads:
        load.start()
    for k in range(K2):
        send1[k] = zs[:, k].reshape(npy, 64, 128).astype(BF)

    pl.semaphore_wait(barrier, npy + npx - 2)

    def y_copy(k, src, dst, ssem, rsem, target, many=True):
        return pltpu.make_async_remote_copy(
            src_ref=src.at[k, target], dst_ref=dst.at[k, mey], send_sem=ssem.at[k],
            recv_sem=rsem.at[k, mey if many else 0], device_id=(mex, target), device_id_type=MESH,
        )

    def y_whole(k, src, dst, ssem, rsem):
        return pltpu.make_async_remote_copy(
            src_ref=src.at[k, pl.ds(0, npy - 1)], dst_ref=dst.at[k, pl.ds(0, npy - 1)], send_sem=ssem.at[k],
            recv_sem=rsem.at[k, 0], device_id=(mex, twin), device_id_type=MESH,
        )

    def y_arrive(k, source):
        pltpu.make_async_remote_copy(
            src_ref=send1.at[k, source], dst_ref=recv1.at[k, source], send_sem=ssem1.at[k],
            recv_sem=rsem1.at[k, source], device_id=(mex, source), device_id_type=MESH,
        ).wait_recv()

    def x_start(k, src, dst, sems):
        for other in x_peers:
            pltpu.make_async_remote_copy(
                src_ref=src.at[k, other], dst_ref=dst.at[k, mex], send_sem=sems.at[k, 0], recv_sem=sems.at[k, 1],
                device_id=(other, mey), device_id_type=MESH,
            ).start()
        dst[k, pl.ds(mex, 1)] = src[k, pl.ds(mex, 1)]

    def x_whole(k, src, dst, sems):
        return pltpu.make_async_remote_copy(
            src_ref=src.at[k, pl.ds(0, npx - 1)], dst_ref=dst.at[k, pl.ds(0, npx - 1)], send_sem=sems.at[k, 0],
            recv_sem=sems.at[k, 1], device_id=(x_peers[0], mey), device_id_type=MESH,
        )

    def y_peers(far_first):
        offsets = sorted(range(1, ny), key=lambda d: min(d, ny - d), reverse=far_first)
        return [lax.rem(my_chip + d, ny) for d in offsets]

    for k in range(K2):
        for chip in y_peers(True):
            for core in range(2):
                y_copy(k, send1, recv1, ssem1, rsem1, chip * 2 + core).start()
        y_copy(k, send1, recv1, ssem1, rsem1, twin).start()
        recv1[k, pl.ds(mey, 1)] = send1[k, pl.ds(mey, 1)]

    for i in range(3):
        loads[i].wait()
    spread = (lax.broadcasted_iota(jnp.int32, (C, C * 8), 1) >> 3 == lax.broadcasted_iota(jnp.int32, (C, C * 8), 0))
    rows = dot(win_ref[...], spread.astype(F32).astype(BF), TN)
    same = lax.broadcasted_iota(jnp.int32, (HID, 8, C * 8), 1) == (
        lax.broadcasted_iota(jnp.int32, (HID, 8, C * 8), 2) & 7
    )
    k1[...] = jnp.where(same, rows[:, None, :], 0.0).reshape(HID * 8, C * 8).astype(BF)
    spread = (
        lax.broadcasted_iota(jnp.int32, (HID, HID * 8), 1) >> 3 == lax.broadcasted_iota(jnp.int32, (HID, HID * 8), 0)
    )
    rows = dot(wout_ref[...], spread.astype(F32).astype(BF), NN)
    same = lax.broadcasted_iota(jnp.int32, (C, 8, HID * 8), 1) == (
        lax.broadcasted_iota(jnp.int32, (C, 8, HID * 8), 2) & 7
    )
    k2[...] = jnp.where(same, rows[:, None, :], 0.0).reshape(C * 8, HID * 8).astype(BF)
    turned = jnp.transpose(jnp.broadcast_to(bin_ref[...], (HID, HID)))
    bias[...] = jnp.broadcast_to(turned[:, None, :], (HID, 8, 128)).reshape(HID * 8, 128)

    def channel(i, carry):
        block = f_ref[:, pl.ds(pl.multiple_of(i * 16, 16), 16), :].astype(F32)
        cells = jnp.concatenate(
            [block[:, :8].reshape(C * 8, 128), block[:, 8:].reshape(C * 8, 128)], axis=1
        ).astype(BF)
        acc = jnp.zeros((C * 8, 256), F32)
        for part in range(4):
            rows = slice(part * 256, part * 256 + 256)
            b = bias[rows]
            hidden = gelu(dot(k1[rows], cells, NN) + jnp.concatenate([b, b], axis=1)).astype(BF)
            acc = acc + dot(k2[:, rows], hidden, NN)
        chan[:, pl.ds(pl.multiple_of(i * 16, 16), 8), :] = acc[:, :128].reshape(C, 8, 128)
        chan[:, pl.ds(pl.multiple_of(i * 16 + 8, 8), 8), :] = acc[:, 128:].reshape(C, 8, 128)
        return carry

    half = npx * XL
    lane = lax.broadcasted_iota(jnp.int32, (1, 128), 1)
    real_lane = (lane & 4) == 0
    sign = jnp.where(real_lane, 1.0, -1.0)

    def swap(v):
        return jnp.where(real_lane, pltpu.roll(v, 124, 1), pltpu.roll(v, 4, 1))

    def along_y(k):
        def part(chip):
            pair = jnp.concatenate([recv1[k, chip * 2], recv1[k, chip * 2 + 1]], axis=1)
            return dot(a2_ref[chip], jnp.concatenate([pair, pair], axis=0), NT)

        y_arrive(k, twin)
        acc = part(my_chip)
        for chip in y_peers(False):
            for core in range(2):
                y_arrive(k, chip * 2 + core)
            acc = acc + part(chip)
        lines = acc[:half] + sign * swap(acc[half:])
        send2[k] = lines.reshape(npx, XL, 128).astype(BF)
        x_start(k, send2, recv2, sems2)

    def mixed(k):
        x_whole(k, send2, recv2, sems2).wait_recv()
        block = recv2[k].astype(F32).reshape(half, 128).astype(BF)
        both = dot(tx_ref[...], block, NN)
        spectra = both[:mx] + sign * swap(both[mx:])
        xpat[...] = dot(e8_ref[...], spectra.astype(BF), NT).reshape(2 * C, 8, mx)

        def mix(c, carry):
            real, imag = carry
            wr = w_ref[0, c].astype(F32).reshape(8, 8, mx)
            wi = w_ref[1, c].astype(F32).reshape(8, 8, mx)
            xr = xpat[c][None]
            xi = xpat[c + C][None]
            return real + xr * wr - xi * wi, imag + xr * wi + xi * wr

        zero = jnp.zeros((8, 8, mx), F32)
        real, imag = lax.fori_loop(0, C, mix, (zero, zero), unroll=4)
        modes = jnp.concatenate([real.reshape(64, mx), imag.reshape(64, mx)], axis=0).astype(BF)
        modes = dot(pick_ref[k], modes, NN).astype(BF)

        both = dot(tix_ref[...], modes, NT)
        cells = both[:half] - sign * swap(both[half:])
        send3[k] = cells.reshape(npx, XL, 128).astype(BF)
        x_start(k, send3, recv3, sems3)

    def back_y(k):
        x_whole(k, send3, recv3, sems3).wait_recv()
        block = recv3[k].astype(F32).reshape(half, 128)
        turned = jnp.concatenate([block, -sign * swap(block)], axis=0)
        turned = jnp.transpose(turned)[:64].astype(BF)

        def cells(chip):
            both = dot(turned, a2_ref[chip], NN).astype(BF)
            send4[k, pl.ds(chip * 2, 1)] = both[:, :128][None]
            send4[k, pl.ds(chip * 2 + 1, 1)] = both[:, 128:][None]

        for chip in y_peers(True):
            cells(chip)
            for core in range(2):
                y_copy(k, send4, recv4, ssem4, rsem4, chip * 2 + core, False).start()
        cells(my_chip)
        y_copy(k, send4, recv4, ssem4, rsem4, twin, False).start()
        recv4[k, pl.ds(mey, 1)] = send4[k, pl.ds(mey, 1)]

    lax.fori_loop(0, 2, channel, 0)
    for i in range(3, 9):
        loads[i].wait()
    along_y(0)
    lax.fori_loop(2, 4, channel, 0)
    along_y(1)
    mixed(0)
    mixed(1)
    back_y(0)
    channel(4, 0)
    back_y(1)
    lax.fori_loop(5, 8, channel, 0)
    for k in range(K2):
        y_whole(k, send1, recv1, ssem1, rsem1).wait_send()
        x_whole(k, send2, recv2, sems2).wait_send()
        x_whole(k, send3, recv3, sems3).wait_send()
    for k in range(K2):
        y_whole(k, send4, recv4, ssem4, rsem4).wait_recv()
        sent.append(y_whole(k, send4, recv4, ssem4, rsem4))
    for copy in sent:
        copy.wait_send()


def finish(npy, recv4, chan, b7_ref, out_hbm, done, sems):
    copies = []
    for g in range(4):
        lines = recv4[:, :, 16 * g : 16 * g + 16, :].reshape(npy * 32, 128)
        values = dot(lines, b7_ref[...], TN)
        for o in range(8):
            total = values[:, 128 * o : 128 * o + 128] + chan[8 * g + o]
            done[8 * g + o] = gelu(total).astype(BF)
        block = pl.ds(8 * g, 8)
        copies.append(pltpu.make_async_copy(done.at[block], out_hbm.at[block], sems.at[g]))
        copies[-1].start()
    for copy in copies:
        copy.wait()


def body(npx, npy, field, spec_weight, w_in, b_in, w_out):
    mx = spec_weight.shape[4]
    a1, a2, tx, tix, b7, e8, pick = tables(npx, npy, mx)
    cells = field.reshape(C, XL * YL, NZ)
    weight = jnp.transpose(spec_weight[0], (0, 1, 2, 4, 5, 3)).reshape(2, C, C * K2, mx)
    vmem = pl.BlockSpec(memory_space=pltpu.VMEM)
    hbm = pl.BlockSpec(memory_space=pltpu.HBM)
    exchange = [pltpu.VMEM((K2, npx, XL, 128), BF)] * 2
    loaded = [
        cells, jnp.asarray(a1), w_in[0], b_in, jnp.transpose(w_out[0]), weight,
        jnp.asarray(a2), jnp.asarray(tx), jnp.asarray(tix), jnp.asarray(e8), jnp.asarray(pick),
    ]
    loaded = [pltpu.with_memory_space_constraint(a, pltpu.HBM) for a in loaded]
    lines, chan = pl.pallas_call(
        functools.partial(kernel, npx, npy),
        out_shape=(
            pltpu.VMEM((K2, npy, 64, 128), BF),
            pltpu.VMEM((C, XL * YL, NZ), F32),
        ),
        in_specs=[hbm] * len(loaded),
        out_specs=(vmem, vmem),
        scratch_shapes=[
            pltpu.VMEM((npy, K2, 8, 8, 128), F32),
            pltpu.VMEM((K2, npy, 64, 128), BF),
            pltpu.VMEM((K2, npy, 64, 128), BF),
            *exchange,
            *exchange,
            pltpu.VMEM((K2, npy, 64, 128), BF),
            *[pltpu.VMEM(a.shape, a.dtype) for a in loaded],
            pltpu.VMEM((HID * 8, C * 8), BF),
            pltpu.VMEM((C * 8, HID * 8), BF),
            pltpu.VMEM((HID * 8, 128), F32),
            pltpu.VMEM((2 * C, 8, mx), F32),
            pltpu.SemaphoreType.DMA((K2,)),
            pltpu.SemaphoreType.DMA((K2, npy)),
            pltpu.SemaphoreType.DMA((K2, 2)),
            pltpu.SemaphoreType.DMA((K2, 2)),
            pltpu.SemaphoreType.DMA((K2,)),
            pltpu.SemaphoreType.DMA((K2, 1)),
            pltpu.SemaphoreType.DMA((14,)),
        ],
        compiler_params=pltpu.CompilerParams(
            collective_id=0, has_side_effects=True, vmem_limit_bytes=32 * 1024 * 1024
        ),
    )(*loaded)
    out = pl.pallas_call(
        functools.partial(finish, npy),
        out_shape=jax.ShapeDtypeStruct((C, XL * YL, NZ), BF),
        in_specs=[vmem] * 3,
        out_specs=hbm,
        scratch_shapes=[pltpu.VMEM((C, XL * YL, NZ), BF), pltpu.SemaphoreType.DMA((4,))],
        compiler_params=pltpu.CompilerParams(vmem_limit_bytes=16 * 1024 * 1024),
    )(lines, chan, jnp.asarray(b7))
    return out.reshape(field.shape)


def solution(mesh):
    in_specs = (
        P(None, "px", "py", None),
        P(None, None, None, None, None, "px", "py"),
        P(),
        P(),
        P(),
    )
    return jax.shard_map(
        functools.partial(body, mesh.shape["px"], mesh.shape["py"]),
        mesh=mesh, in_specs=in_specs, out_specs=P(None, "px", "py", None), check_vma=False,
    )
```

time: 59.5 us -> 56.2 us (0.945)
  Pallas kernels: 59.4 us -> 56 us
    pallas_call x1, Pallas kernels: 57.5 us -> 54.1 us  [body(): pl.pallas_call(functools.partial(kernel, npx, npy), out_shape=(pltpu.VMEM...]
where the time goes in v6:
time: 56.2 us; the launch traced here: 56 us
  Pallas kernels  56 us (100%)
    pallas_call x1, Pallas kernels, body(): pl.pallas_call(functools.partial(kernel, npx, npy), out_shape=(pltpu.VMEM...  54.1 us
    pallas_call x1, Pallas kernels, body(): pl.pallas_call(functools.partial(finish, npy), out_shape=jax.ShapeDtypeSt...  1.93 us

profile of v6, /device:TPU:1, one launch (start us, length us, event | category | flops | bytes accessed | tf_op | source)
XLA Modules:
  0.0 56.0 jit_solution(6202578254843064392)
XLA Ops:
  0.0 0.0 copy-start
  0.0 54.1 %shard_map.118 = (bf16[2,16,64,128]{3,2,1,0:T(8,128)(2,1)S(1)}, f32[32,128,128]{2,1,0:T(8,128)S(1)}) custom-call(bf16[32,128,128]{2,1,0:T(8,128)(2,1)} %bitcast.11, bf16[2,256,256]{2,1,0:T(8,128)(2,1)} %constant.14.clone.a1_hbm, bf16[32,128]{1,0:T(8,128)(2,1)} %bitcast.13, f32[1,128]{1,0:T(1,128)} %bin_hbm.1, bf16[32,128]{1,0:T(8,128)(2,1)} %bitcast.14, ...), custom_call_target="tpu_custom_call" | custom-call | tf_op jit(solution)/shard_map/pallas_call | solution.py:343
  54.1 0.0 copy-done
  54.1 1.9 %shard_map.119 = bf16[32,128,128]{2,1,0:T(8,128)(2,1)} custom-call(bf16[2,16,64,128]{3,2,1,0:T(8,128)(2,1)S(1)} %get-tuple-element.7.recv4, f32[32,128,128]{2,1,0:T(8,128)S(1)} %get-tuple-element.8.chan, bf16[512,1024]{1,0:T(8,128)(2,1)S(1)} %copy-done), custom_call_target="tpu_custom_call" | custom-call | tf_op jit(solution)/shard_map/pallas_call | solution.py:375
Async XLA Ops:
  0.0 54.1 %copy-start = (bf16[512,1024]{1,0:T(8,128)(2,1)S(1)}, bf16[512,1024]{1,0:T(8,128)(2,1)}, u32[]{:S(2)}) copy-start(bf16[512,1024]{1,0:T(8,128)(2,1)} %constant.20.clone.b7_ref) | copy-start | bytes 3145732

commit v7 on v6

--- a/solution.py
+++ b/solution.py
@@ -41,8 +41,8 @@
     nx, ny, my, mz = XL * npx, YL * npy, npx, K2 * npy
     ang = angles(np.arange(NZ), np.arange(mz), NZ)
     fwd = np.stack([np.cos(ang), -np.sin(ang)]) * 0.125
-    fwd = fwd.reshape(2, NZ, npy, K2).transpose(2, 3, 0, 1)
-    a1 = np.zeros((2, npy, K2, 2, 4, 2, NZ))
+    fwd = fwd.reshape(2, NZ, npy, K2).transpose(3, 2, 0, 1)
+    a1 = np.zeros((2, K2, npy, 2, 4, 2, NZ))
     for q in range(2):
         for c in range(2):
             a1[q, :, :, :, 2 * q + c, c, :] = fwd
@@ -64,7 +64,7 @@
     b7 = np.zeros((K2, npy, 2, 2, 4, 8, NZ))
     for o in range(8):
         b7[:, :, o // 4, :, o % 4, o, :] = inv
-    b7 = b7.reshape(npy * 32, 8 * NZ)
+    b7 = b7.reshape(K2, npy * 16, 8 * NZ)
     e8 = np.zeros((2, C, 8, 2, C // 4, 2, 4))
     for c in range(C):
         for ri in range(2):
@@ -91,10 +91,10 @@
 
 def kernel(
     npx, npy,
-    f_hbm, a1_hbm, win_hbm, bin_hbm, wout_hbm, w_hbm, a2_hbm, tx_hbm, tix_hbm, e8_hbm, pick_hbm,
+    f_hbm, a1_hbm, win_hbm, bin_hbm, wout_hbm, w_hbm, a2_hbm, tx_hbm, tix_hbm, e8_hbm, pick_hbm, b7_hbm,
     recv4, chan,
     zs, send1, recv1, send2, recv2, send3, recv3, send4,
-    f_ref, a1_ref, win_ref, bin_ref, wout_ref, w_ref, a2_ref, tx_ref, tix_ref, e8_ref, pick_ref,
+    f_ref, a1_ref, win_ref, bin_ref, wout_ref, w_ref, a2_ref, tx_ref, tix_ref, e8_ref, pick_ref, b7_ref,
     k1, k2, bias, xpat,
     ssem1, rsem1, sems2, sems3, ssem4, rsem4, tsem,
 ):
@@ -114,7 +114,7 @@
         load(1 + i, f_hbm.at[pl.ds(i * 8, 8)], f_ref.at[pl.ds(i * 8, 8)]) for i in range(4)
     ]
     pairs = [(win_hbm, win_ref), (bin_hbm, bin_ref), (wout_hbm, wout_ref), (a2_hbm, a2_ref), (tx_hbm, tx_ref),
-             (e8_hbm, e8_ref), (w_hbm, w_ref), (tix_hbm, tix_ref), (pick_hbm, pick_ref)]
+             (e8_hbm, e8_ref), (w_hbm, w_ref), (tix_hbm, tix_ref), (pick_hbm, pick_ref), (b7_hbm, b7_ref)]
     loads = [load(5 + i, src, dst) for i, (src, dst) in enumerate(pairs)]
     barrier = pltpu.get_barrier_semaphore()
 
@@ -127,21 +127,22 @@
     for peer in x_peers:
         pl.semaphore_signal(barrier, inc=1, device_id=(peer, mey), device_id_type=MESH)
 
-    def forward_z(g, carry):
-        f4 = f_ref[pl.ds(g * 4, 4)]
-        acc = dot(a1_ref[0], jnp.concatenate([f4[0], f4[1]], axis=1), NT)
-        acc = acc + dot(a1_ref[1], jnp.concatenate([f4[2], f4[3]], axis=1), NT)
-        zs[:, :, pl.ds(g, 1)] = acc.reshape(npy, K2, 1, 8, 128)
-        return carry
+    def forward_z(k, groups):
+        def four(g, carry):
+            f4 = f_ref[pl.ds(g * 4, 4)]
+            rows = slice(k * npy * 8, (k + 1) * npy * 8)
+            acc = dot(a1_ref[0, rows], jnp.concatenate([f4[0], f4[1]], axis=1), NT)
+            acc = acc + dot(a1_ref[1, rows], jnp.concatenate([f4[2], f4[3]], axis=1), NT)
+            zs[:, pl.ds(g, 1)] = acc.reshape(npy, 1, 8, 128)
+            return carry
+
+        lax.fori_loop(groups[0], groups[1], four, 0, unroll=2)
 
     cells_in[0].wait()
     for i in range(4):
         cells_in[1 + i].wait()
-        lax.fori_loop(2 * i, 2 * i + 2, forward_z, 0, unroll=2)
-    for load in loads:
-        load.start()
-    for k in range(K2):
-        send1[k] = zs[:, k].reshape(npy, 64, 128).astype(BF)
+        forward_z(0, (2 * i, 2 * i + 2))
+    send1[0] = zs[...].reshape(npy, 64, 128).astype(BF)
 
     pl.semaphore_wait(barrier, npy + npx - 2)
 
@@ -187,6 +188,11 @@
                 y_copy(k, send1, recv1, ssem1, rsem1, chip * 2 + core).start()
         y_copy(k, send1, recv1, ssem1, rsem1, twin).start()
         recv1[k, pl.ds(mey, 1)] = send1[k, pl.ds(mey, 1)]
+        if k == 0:
+            for load in loads:
+                load.start()
+            forward_z(1, (0, C // 4))
+            send1[1] = zs[...].reshape(npy, 64, 128).astype(BF)
 
     for i in range(3):
         loads[i].wait()
@@ -290,7 +296,7 @@
         recv4[k, pl.ds(mey, 1)] = send4[k, pl.ds(mey, 1)]
 
     lax.fori_loop(0, 2, channel, 0)
-    for i in range(3, 9):
+    for i in range(3, 10):
         loads[i].wait()
     along_y(0)
     lax.fori_loop(2, 4, channel, 0)
@@ -305,18 +311,27 @@
         y_whole(k, send1, recv1, ssem1, rsem1).wait_send()
         x_whole(k, send2, recv2, sems2).wait_send()
         x_whole(k, send3, recv3, sems3).wait_send()
+    y_whole(0, send4, recv4, ssem4, rsem4).wait_recv()
+    for g in range(4):
+        values = back_z(recv4, 0, b7_ref, g)
+        for o in range(8):
+            chan[8 * g + o] = chan[8 * g + o] + values[:, 128 * o : 128 * o + 128]
+    y_whole(1, send4, recv4, ssem4, rsem4).wait_recv()
     for k in range(K2):
-        y_whole(k, send4, recv4, ssem4, rsem4).wait_recv()
         sent.append(y_whole(k, send4, recv4, ssem4, rsem4))
     for copy in sent:
         copy.wait_send()
 
 
-def finish(npy, recv4, chan, b7_ref, out_hbm, done, sems):
+def back_z(lines, k, table, g):
+    rows = lines[k, :, 16 * g : 16 * g + 16, :]
+    return dot(rows.reshape(rows.shape[0] * 16, 128), table[...], TN)
+
+
+def finish(recv4, chan, b7_ref, out_hbm, done, sems):
     copies = []
     for g in range(4):
-        lines = recv4[:, :, 16 * g : 16 * g + 16, :].reshape(npy * 32, 128)
-        values = dot(lines, b7_ref[...], TN)
+        values = back_z(recv4, 1, b7_ref, g)
         for o in range(8):
             total = values[:, 128 * o : 128 * o + 128] + chan[8 * g + o]
             done[8 * g + o] = gelu(total).astype(BF)
@@ -337,7 +352,7 @@
     exchange = [pltpu.VMEM((K2, npx, XL, 128), BF)] * 2
     loaded = [
         cells, jnp.asarray(a1), w_in[0], b_in, jnp.transpose(w_out[0]), weight,
-        jnp.asarray(a2), jnp.asarray(tx), jnp.asarray(tix), jnp.asarray(e8), jnp.asarray(pick),
+        jnp.asarray(a2), jnp.asarray(tx), jnp.asarray(tix), jnp.asarray(e8), jnp.asarray(pick), jnp.asarray(b7[0]),
     ]
     loaded = [pltpu.with_memory_space_constraint(a, pltpu.HBM) for a in loaded]
     lines, chan = pl.pallas_call(
@@ -349,7 +364,7 @@
         in_specs=[hbm] * len(loaded),
         out_specs=(vmem, vmem),
         scratch_shapes=[
-            pltpu.VMEM((npy, K2, 8, 8, 128), F32),
+            pltpu.VMEM((npy, 8, 8, 128), F32),
             pltpu.VMEM((K2, npy, 64, 128), BF),
             pltpu.VMEM((K2, npy, 64, 128), BF),
             *exchange,
@@ -366,20 +381,20 @@
             pltpu.SemaphoreType.DMA((K2, 2)),
             pltpu.SemaphoreType.DMA((K2,)),
             pltpu.SemaphoreType.DMA((K2, 1)),
-            pltpu.SemaphoreType.DMA((14,)),
+            pltpu.SemaphoreType.DMA((15,)),
         ],
         compiler_params=pltpu.CompilerParams(
             collective_id=0, has_side_effects=True, vmem_limit_bytes=32 * 1024 * 1024
         ),
     )(*loaded)
     out = pl.pallas_call(
-        functools.partial(finish, npy),
+        finish,
         out_shape=jax.ShapeDtypeStruct((C, XL * YL, NZ), BF),
         in_specs=[vmem] * 3,
         out_specs=hbm,
         scratch_shapes=[pltpu.VMEM((C, XL * YL, NZ), BF), pltpu.SemaphoreType.DMA((4,))],
         compiler_params=pltpu.CompilerParams(vmem_limit_bytes=16 * 1024 * 1024),
-    )(lines, chan, jnp.asarray(b7))
+    )(lines, chan, jnp.asarray(b7[1]))
     return out.reshape(field.shape)
 
 

time: 56.2 us -> 55.8 us (level)
  no operation moved by 1% of the time
where the time goes in v7:
time: 55.8 us; the launch traced here: 55.7 us
  Pallas kernels  55.7 us (100%)
    pallas_call x1, Pallas kernels, body(): pl.pallas_call(functools.partial(kernel, npx, npy), out_shape=(pltpu.VMEM...  54 us
    pallas_call x1, Pallas kernels, body(): pl.pallas_call(finish, out_shape=jax.ShapeDtypeStruct((C, XL * YL, NZ), B...  1.71 us

profile of v7, /device:TPU:1, one launch (start us, length us, event | category | flops | bytes accessed | tf_op | source)
XLA Modules:
  0.0 55.7 jit_solution(16796485555790294192)
XLA Ops:
  0.0 0.0 copy-start
  0.0 54.0 %shard_map.127 = (bf16[2,16,64,128]{3,2,1,0:T(8,128)(2,1)S(1)}, f32[32,128,128]{2,1,0:T(8,128)S(1)}) custom-call(bf16[32,128,128]{2,1,0:T(8,128)(2,1)} %bitcast.11, bf16[2,256,256]{2,1,0:T(8,128)(2,1)} %constant.16.clone.a1_hbm, bf16[32,128]{1,0:T(8,128)(2,1)} %bitcast.13, f32[1,128]{1,0:T(1,128)} %bin_hbm.1, bf16[32,128]{1,0:T(8,128)(2,1)} %bitcast.14, ...), custom_call_target="tpu_custom_call" | custom-call | tf_op jit(solution)/shard_map/pallas_call | solution.py:358
  54.0 0.0 copy-done
  54.0 1.7 %shard_map.128 = bf16[32,128,128]{2,1,0:T(8,128)(2,1)} custom-call(bf16[2,16,64,128]{3,2,1,0:T(8,128)(2,1)S(1)} %get-tuple-element.7.recv4, f32[32,128,128]{2,1,0:T(8,128)S(1)} %get-tuple-element.8.chan, bf16[256,1024]{1,0:T(8,128)(2,1)S(1)} %copy-done), custom_call_target="tpu_custom_call" | custom-call | tf_op jit(solution)/shard_map/pallas_call | solution.py:390
Async XLA Ops:
  0.0 54.0 %copy-start = (bf16[256,1024]{1,0:T(8,128)(2,1)S(1)}, bf16[256,1024]{1,0:T(8,128)(2,1)}, u32[]{:S(2)}) copy-start(bf16[256,1024]{1,0:T(8,128)(2,1)} %constant.23.clone.b7_ref) | copy-start | bytes 1572868

commit v8 on v7

--- a/solution.py
+++ b/solution.py
@@ -299,12 +299,12 @@
     for i in range(3, 10):
         loads[i].wait()
     along_y(0)
-    lax.fori_loop(2, 4, channel, 0)
+    channel(2, 0)
+    mixed(0)
     along_y(1)
-    mixed(0)
     mixed(1)
     back_y(0)
-    channel(4, 0)
+    lax.fori_loop(3, 5, channel, 0)
     back_y(1)
     lax.fori_loop(5, 8, channel, 0)
     for k in range(K2):

time: 55.8 us -> 59.2 us (1.061)
  Pallas kernels: 55.7 us -> 59.1 us
    pallas_call x1, Pallas kernels: 54 us -> 57.4 us  [body(): pl.pallas_call(functools.partial(kernel, npx, npy), out_shape=(pltpu.VMEM...]
where the time goes in v8:
time: 59.2 us; the launch traced here: 59.1 us
  Pallas kernels  59.1 us (100%)
    pallas_call x1, Pallas kernels, body(): pl.pallas_call(functools.partial(kernel, npx, npy), out_shape=(pltpu.VMEM...  57.4 us
    pallas_call x1, Pallas kernels, body(): pl.pallas_call(finish, out_shape=jax.ShapeDtypeStruct((C, XL * YL, NZ), B...  1.71 us

profile of v8, /device:TPU:1, one launch (start us, length us, event | category | flops | bytes accessed | tf_op | source)
XLA Modules:
  0.0 59.1 jit_solution(10925962653680899250)
XLA Ops:
  0.0 0.0 copy-start
  0.0 57.4 %shard_map.127 = (bf16[2,16,64,128]{3,2,1,0:T(8,128)(2,1)S(1)}, f32[32,128,128]{2,1,0:T(8,128)S(1)}) custom-call(bf16[32,128,128]{2,1,0:T(8,128)(2,1)} %bitcast.11, bf16[2,256,256]{2,1,0:T(8,128)(2,1)} %constant.16.clone.a1_hbm, bf16[32,128]{1,0:T(8,128)(2,1)} %bitcast.13, f32[1,128]{1,0:T(1,128)} %bin_hbm.1, bf16[32,128]{1,0:T(8,128)(2,1)} %bitcast.14, ...), custom_call_target="tpu_custom_call" | custom-call | tf_op jit(solution)/shard_map/pallas_call | solution.py:358
  57.4 0.0 copy-done
  57.4 1.7 %shard_map.128 = bf16[32,128,128]{2,1,0:T(8,128)(2,1)} custom-call(bf16[2,16,64,128]{3,2,1,0:T(8,128)(2,1)S(1)} %get-tuple-element.7.recv4, f32[32,128,128]{2,1,0:T(8,128)S(1)} %get-tuple-element.8.chan, bf16[256,1024]{1,0:T(8,128)(2,1)S(1)} %copy-done), custom_call_target="tpu_custom_call" | custom-call | tf_op jit(solution)/shard_map/pallas_call | solution.py:390
Async XLA Ops:
  0.0 57.4 %copy-start = (bf16[256,1024]{1,0:T(8,128)(2,1)S(1)}, bf16[256,1024]{1,0:T(8,128)(2,1)}, u32[]{:S(2)}) copy-start(bf16[256,1024]{1,0:T(8,128)(2,1)} %constant.23.clone.b7_ref) | copy-start | bytes 1572868
